TPU v7x, 256 devices: a whole 4x4x8 slice. The times are simulated.
256 devices in a mesh: sub: 2 (over x_hi), row: 8 (over y, core), col: 16 (over x_lo, z).
Axes of the slice: x: 4 (x_hi: 2, x_lo: 2; x = x_hi * 2 + x_lo), y: 4, z: 8, core: 2. Of those that a mesh axis runs over, the one named last changes fastest.
Arguments:
- child_update: float32 [2, 4096, 4096], P('sub', 'row', 'col'), as said below
- child_coupling: bfloat16 [2, 4096, 2048], P('sub', 'row', 'col'), may hold values from -0.0625 to 0.0625
- pivot_inverse: bfloat16 [2, 2048, 2048], P('sub', 'col'), as said below
- child_map: int32 [2, 16], replicated, may hold values from 0 to 31, as said below
- parent_front: float32 [8192, 8192], P(('sub', 'row'), 'col'), as said below
- block_pattern: int32 [32, 32], P(('sub', 'row'), 'col'), may hold values from 0 to 1, as said below
Outputs:
- factored: float32 [8192, 8192], P(('sub', 'row'), 'col')
Inputs may be any that keep to these rules, and one draw needn't show every extreme that they name: child_map[s, b] is the parent block that block b of child s lands in, for rows and columns alike; one child's values are distinct, and child_map[s, b] // 2 == b. `block_pattern`: Symmetric, with ones on the diagonal and in every block row and block column below 2. `child_update`: each child's matrix is symmetric. `parent_front`: Symmetric. `pivot_inverse`: each child's matrix is lower triangular with a nonzero diagonal.
All inputs are finite; a program needn't handle non-finite values.
Results may differ from a plain program's by a relative error of at most 0.0019.
Values may be sent and summed in bfloat16 or wider, within the bound.
A program may use at most 64 MiB of HBM per device.

v0:
```python
import jax
import jax.numpy as jnp
from jax import lax
from jax.sharding import PartitionSpec as P

BLK = 256
PSTEPS = 2
NBC = 16
KP = 512


highest = lax.Precision.HIGHEST


def broadcast(x, axis, root):
    mine = lax.axis_index(axis) == root
    return lax.psum(jnp.where(mine, x, jnp.zeros_like(x)), axis)


def from_partner(x, axis, stride):
    return lax.ppermute(x, axis, [(i, i ^ 1 << stride) for i in range(lax.axis_size(axis))])


def factor_pivot(pivot_block, usable):
    order_size = pivot_block.shape[0]
    identity = jnp.eye(order_size, dtype=jnp.float32)
    safe_block = jnp.where(usable, pivot_block, identity)
    lower_pivot = jnp.linalg.cholesky(safe_block)
    inverse = jax.scipy.linalg.solve_triangular(lower_pivot, identity, lower=True)
    return (lower_pivot, inverse)


def times_inverse(columns, inverse):
    return lax.dot_general(
        columns,
        inverse,
        (((1,), (1,)), ((), ())),
        precision=highest,
        preferred_element_type=jnp.float32,
    )


def outer_update(left_rows, right_rows):
    return lax.dot_general(
        left_rows,
        right_rows,
        (((1,), (1,)), ((), ())),
        precision=highest,
        preferred_element_type=jnp.float32,
    )


def local(child_update, child_coupling, pivot_inverse, child_map, parent_front, block_pattern):
    update_local = child_update[0]
    coupling_local = child_coupling[0]
    inverse_rows = pivot_inverse[0]
    rows_here = update_local.shape[0]
    width_here = update_local.shape[1]
    panel_block = lax.dot_general(
        lax.all_gather(coupling_local, "col", axis=1, tiled=True),
        inverse_rows,
        (((1,), (1,)), ((), ())),
        preferred_element_type=jnp.float32,
    ).astype(jnp.bfloat16)
    panel_rows = lax.all_gather(panel_block, "col", axis=1, tiled=True)
    col_index = lax.axis_index("col")
    start_row = col_index * width_here
    owner_row = start_row // rows_here
    offset = start_row - owner_row * rows_here
    slab_rows = lax.dynamic_slice_in_dim(panel_rows, offset, width_here, 0)
    panel_cols = broadcast(slab_rows, "row", owner_row)
    schur_part = update_local - lax.dot_general(
        panel_rows, panel_cols, (((1,), (1,)), ((), ())), preferred_element_type=jnp.float32
    )
    column_slab = lax.all_gather(schur_part, "row", axis=0, tiled=True)
    child_blocks = column_slab.reshape(NBC, BLK, width_here)
    local_rows, local_cols = parent_front.shape
    group_rows = local_rows // BLK
    group_cols = local_cols // BLK
    child_cols = width_here // BLK
    sub_index = lax.axis_index("sub")
    row_count = lax.axis_size("row")
    group_here = lax.axis_index(("sub", "row"))
    group_other = group_here + (1 - 2 * sub_index) * row_count
    own_map = lax.dynamic_index_in_dim(child_map, sub_index, 0, keepdims=False)
    other_map = lax.dynamic_index_in_dim(child_map, 1 - sub_index, 0, keepdims=False)

    def select_rows(mapping, group_id):
        wanted = group_id * group_rows + jnp.arange(group_rows, dtype=jnp.int32)
        onehot = (mapping[None, :] == wanted[:, None]).astype(jnp.float32)
        return jnp.einsum("ib,bxy->ixy", onehot, child_blocks, precision=highest)

    def place_columns(rows_part, mapping):
        first_block = col_index * child_cols
        targets = (
            lax.dynamic_slice_in_dim(mapping, first_block, child_cols) - col_index * group_cols
        )
        onehot = (targets[:, None] == jnp.arange(group_cols, dtype=jnp.int32)[None, :]).astype(
            jnp.float32
        )
        shaped = rows_part.reshape(group_rows, BLK, child_cols, BLK)
        return jnp.einsum("ixjy,jk->ixky", shaped, onehot, precision=highest).reshape(
            local_rows, local_cols
        )

    own_rows = select_rows(own_map, group_here)
    other_rows = from_partner(select_rows(own_map, group_other), "sub", 0)
    pattern = block_pattern.astype(jnp.float32)
    masked = (
        parent_front.reshape(group_rows, BLK, group_cols, BLK) * pattern[:, None, :, None]
    ).reshape(local_rows, local_cols)
    current = masked + place_columns(own_rows, own_map) + place_columns(other_rows, other_map)
    row_start = group_here * local_rows
    global_rows = row_start + jnp.arange(local_rows, dtype=jnp.int32)
    global_cols = col_index * local_cols + jnp.arange(local_cols, dtype=jnp.int32)
    first_col = col_index == 0
    fan_ratio = lax.axis_size(("sub", "row")) // lax.axis_size("col")
    factored_list = []
    for step_index in range(PSTEPS):
        edge_low = step_index * BLK
        edge_high = edge_low + BLK
        corner = current[edge_low:edge_high, edge_low:edge_high]
        pivot_block = broadcast(corner.astype(jnp.bfloat16), ("sub", "row"), 0).astype(corner.dtype)
        lower_pivot, inverse = factor_pivot(pivot_block, first_col)
        column = current[:, edge_low:edge_high]
        product = times_inverse(column, inverse)
        beneath = (global_rows >= edge_high)[:, None]
        below_rows = jnp.where(beneath, product, 0.0)
        across = broadcast(below_rows, "col", 0)
        pieces = broadcast(across, ("sub", "row"), col_index * fan_ratio + 0)
        current = current - outer_update(across, pieces)
        placed = lax.dynamic_update_slice(
            jnp.zeros((local_rows, BLK), jnp.float32), lower_pivot, (edge_low, 0)
        )
        inside = ((global_rows >= edge_low) & (global_rows < edge_high))[:, None]
        factored_list.append(jnp.where(beneath, product, jnp.where(inside, placed, column)))
    finished = jnp.concatenate(factored_list, axis=1)
    merged = jnp.where(first_col, finished, current)
    current = merged
    upper_mask = (global_rows[:, None] < KP) & (global_cols[None, :] > global_rows[:, None])
    return jnp.where(upper_mask, 0.0, current)


def solution(mesh):
    return jax.shard_map(
        local,
        mesh=mesh,
        in_specs=(
            P("sub", "row", "col"),
            P("sub", "row", "col"),
            P("sub", "col", None),
            P(),
            P(("sub", "row"), "col"),
            P(("sub", "row"), "col"),
        ),
        out_specs=P(("sub", "row"), "col"),
        check_vma=False,
    )
```

profile of v0, /device:TPU:1, one launch (start us, length us, event | category | flops | bytes accessed | tf_op | source)
XLA Modules:
  0.0 1299.9 jit_solution(8381830002629955944)
XLA Ops:
  7.3 67.9 %all-gather.9.cloned.1.call-done = bf16[1,512,2048]{2,1,0:T(8,128)(2,1)} async-done(((bf16[1,512,128]{2,1,0:T(8,128)(2,1)}), bf16[1,512,2048]{2,1,0:T(8,128)(2,1)}) %all-gather.9.cloned.1.call-update) | async-done | bytes 2097168 | tf_op jit(solution)/shard_map/all_gather | solution.py:60
  75.2 3.0 fusion.6
  78.3 71.9 %all-gather.5.cloned.1.call-done = bf16[512,2048]{1,0:T(8,128)(2,1)} async-done(((bf16[512,128]{1,0:T(8,128)(2,1)}), bf16[512,2048]{1,0:T(8,128)(2,1)}) %all-gather.5.cloned.1.call-update) | async-done | bytes 2097168 | tf_op jit(solution)/shard_map/all_gather | solution.py:65
  150.2 2.4 dynamic-slice_select_fusion
  152.7 75.3 %all-reduce.11.cloned.1.call-done = bf16[256,2048]{1,0:T(8,128)(2,1)} async-done(((bf16[256,2048]{1,0:T(8,128)(2,1)}), bf16[256,2048]{1,0:T(8,128)(2,1)}) %all-reduce.11.cloned.1.call-update) | async-done | bytes 1048592 | tf_op jit(solution)/shard_map/psum | solution.py:17
  228.0 3.4 convolution_subtract_fusion.2
  235.4 32.6 %all-gather.7.cloned.1.call-done = f32[4096,256]{1,0:T(8,128)} async-done(((f32[512,256]{1,0:T(8,128)}), f32[4096,256]{1,0:T(8,128)}) %all-gather.7.cloned.1.call-update) | async-done | bytes 4194320 | tf_op jit(solution)/shard_map/all_gather | solution.py:75
  268.0 5.5 copy.23
  273.5 6.0 fusion
  279.5 2.8 collective-permute-start
  282.3 1.6 fusion.49
  285.2 9.1 collective-permute-done
  296.1 1.7 add_add_fusion
  298.9 141.6 %all-reduce.13.cloned.1.call-done = bf16[256,256]{0,1:T(8,128)(2,1)} async-done(((bf16[256,256]{0,1:T(8,128)(2,1)}), bf16[256,256]{0,1:T(8,128)(2,1)}) %all-reduce.13.cloned.1.call-update) | async-done | bytes 131088 | tf_op jit(solution)/shard_map/psum | solution.py:17
  442.5 11.7 cholesky.130
  454.4 9.8 custom-call.13
  464.8 11.7 cholesky.147
  478.8 15.3 %while.4 = (s32[]{:T(128)}, f32[256,256]{0,1:T(8,128)S(1)}, s32[2,2]{1,0:T(2,128)S(1)}, f32[2,128,128]{2,1,0:T(8,128)S(1)}, s32[]{:T(128)}) while((s32[]{:T(128)}, f32[256,256]{0,1:T(8,128)S(1)}, s32[2,2]{1,0:T(2,128)S(1)}, f32[2,128,128]{2,1,0:T(8,128)S(1)}, s32[]{:T(128)}) %tuple.50), condition=%wide.while_cond, body=%wide.while_body.sunk | while | flops 2 | bytes 393321 | solution.py:29
  494.1 19.7 %custom-call.14 = f32[2,128,128]{1,2,0:T(8,128)S(1)} custom-call(f32[2,128,128]{2,1,0:T(8,128)S(1)} %get-tuple-element.21), custom_call_target="InvertDiagBlocksLowerTriangular" | custom-call | tf_op jit(solution)/shard_map/jit(_solve_triangular)/triangular_solve | solution.py:29
  516.3 126.5 %all-reduce.15.cloned.1.call-done = f32[512,256]{0,1:T(8,128)} async-done(((f32[512,256]{0,1:T(8,128)}), f32[512,256]{0,1:T(8,128)}) %all-reduce.15.cloned.1.call-update) | async-done | bytes 524304 | tf_op jit(solution)/shard_map/psum | solution.py:17
  643.8 153.0 %all-reduce.17.cloned.1.call-done = f32[512,256]{0,1:T(8,128)} async-done(((f32[512,256]{0,1:T(8,128)}), f32[512,256]{0,1:T(8,128)}) %all-reduce.17.cloned.1.call-update) | async-done | bytes 524304 | tf_op jit(solution)/shard_map/psum | solution.py:17
  796.8 2.3 convolution_subtract_fusion.1
  799.8 142.9 %all-reduce.19.cloned.1.call-done = bf16[256,256]{0,1:T(8,128)(2,1)} async-done(((bf16[256,256]{0,1:T(8,128)(2,1)}), bf16[256,256]{0,1:T(8,128)(2,1)}) %all-reduce.19.cloned.1.call-update) | async-done | bytes 131088 | tf_op jit(solution)/shard_map/psum | solution.py:17
  944.7 11.7 cholesky.164
  956.6 9.8 custom-call.15
  967.0 11.7 cholesky.181
  981.5 4.4 while.5
  986.0 19.7 %custom-call.16 = f32[2,128,128]{1,2,0:T(8,128)S(1)} custom-call(f32[2,128,128]{2,1,0:T(8,128)S(1)} %get-tuple-element.22), custom_call_target="InvertDiagBlocksLowerTriangular" | custom-call | tf_op jit(solution)/shard_map/jit(_solve_triangular)/triangular_solve | solution.py:29
  1006.7 1.7 select_select_fusion.1
  1008.4 126.6 %all-reduce.21.cloned.1.call-done = f32[512,256]{0,1:T(8,128)} async-done(((f32[512,256]{0,1:T(8,128)}), f32[512,256]{0,1:T(8,128)}) %all-reduce.21.cloned.1.call-update) | async-done | bytes 524304 | tf_op jit(solution)/shard_map/psum | solution.py:17
  1136.0 153.0 %all-reduce.23.cloned.1.call-done = f32[512,256]{0,1:T(8,128)} async-done(((f32[512,256]{0,1:T(8,128)}), f32[512,256]{0,1:T(8,128)}) %all-reduce.23.cloned.1.call-update) | async-done | bytes 524304 | tf_op jit(solution)/shard_map/psum | solution.py:17
  1288.9 2.6 fusion.5
  (121 shorter events, 31.3 us)
Async XLA Ops:
  6.5 68.7 %copy-start = (bf16[1,128,2048]{2,1,0:T(8,128)(2,1)S(1)}, bf16[1,128,2048]{2,1,0:T(8,128)(2,1)}, u32[]{:S(2)}) copy-start(bf16[1,128,2048]{2,1,0:T(8,128)(2,1)} %param.11) | copy-start | bytes 1572868
  6.5 221.4 %copy-start.4 = (f32[1,512,256]{2,1,0:T(8,128)S(1)}, f32[1,512,256]{2,1,0:T(8,128)}, u32[]{:S(2)}) copy-start(f32[1,512,256]{2,1,0:T(8,128)} %param.9) | copy-start | bytes 1572868
  6.5 68.7 %all-gather.9.cloned.1.call-start = ((), (), s32[]{:S(2)}) async-start(), calls=%async_computation.9 | async-start | bytes 2228224 | tf_op jit(solution)/shard_map/all_gather | solution.py:60
  7.3 143.0 %all-gather.5.cloned.1.call-start = ((), (), s32[]{:S(2)}) async-start(), calls=%async_computation | async-start | bytes 2228224 | tf_op jit(solution)/shard_map/all_gather | solution.py:65
  78.2 153.3 %copy-start.5 = (s32[2,16]{1,0:T(2,128)S(1)}, s32[2,16]{1,0:T(2,128)}, u32[]{:S(2)}) copy-start(s32[2,16]{1,0:T(2,128)} %param.12) | copy-start | bytes 388
  78.2 155.3 %copy-start.6 = (s32[2,2]{1,0:T(2,128)S(1)}, s32[2,2]{1,0:T(2,128)}, u32[]{:S(2)}) copy-start(s32[2,2]{1,0:T(2,128)} %param.14) | copy-start | bytes 52
  78.2 149.8 %all-reduce.11.cloned.1.call-start = ((), (), s32[]{:S(2)}) async-start(), calls=%async_computation.1 | async-start | bytes 2097152 | tf_op jit(solution)/shard_map/psum | solution.py:17
  152.6 81.3 %copy-start.3 = (f32[512,512]{1,0:T(8,128)S(1)}, f32[512,512]{1,0:T(8,128)}, u32[]{:S(2)}) copy-start(f32[512,512]{1,0:T(8,128)} %param.13) | copy-start | bytes 3145732
  152.7 115.3 %all-gather.7.cloned.1.call-start = ((), (), s32[]{:S(2)}) async-start(), calls=%async_computation.2 | async-start | bytes 4718592 | tf_op jit(solution)/shard_map/all_gather | solution.py:75
  231.4 209.1 %all-reduce.13.cloned.1.call-start = ((), (), s32[]{:S(2)}) async-start(), calls=%async_computation.3 | async-start | bytes 262144 | tf_op jit(solution)/shard_map/psum | solution.py:17
  273.5 8.8 copy-start.1
  279.5 14.9 %collective-permute-start = (f32[2,256,256]{2,0,1:T(2,128)S(1)}, f32[2,256,256]{2,0,1:T(2,128)S(1)}, u32[]{:S(2)}, u32[]{:S(2)}) collective-permute-start(f32[2,256,256]{2,0,1:T(2,128)S(1)} %fusion), channel_id=1, source_target_pairs={{0,128},{128,0},{1,129},{129,1},{2,130},{130,2},{3,131},{131,3},{4... | collective-permute-start | bytes 1572872 | tf_op jit(solution)/shard_map/ppermute | solution.py:21
  294.9 1.2 copy-start.2
  298.5 344.4 %all-reduce.15.cloned.1.call-start = ((), (), s32[]{:S(2)}) async-start(), calls=%async_computation.4 | async-start | bytes 1048576 | tf_op jit(solution)/shard_map/psum | solution.py:17
  516.3 280.5 %all-reduce.17.cloned.1.call-start = ((), (), s32[]{:S(2)}) async-start(), calls=%async_computation.5 | async-start | bytes 1048576 | tf_op jit(solution)/shard_map/psum | solution.py:17
  643.7 298.9 %all-reduce.19.cloned.1.call-start = ((), (), s32[]{:S(2)}) async-start(), calls=%async_computation.6 | async-start | bytes 262144 | tf_op jit(solution)/shard_map/psum | solution.py:17
  799.7 335.3 %all-reduce.21.cloned.1.call-start = ((), (), s32[]{:S(2)}) async-start(), calls=%async_computation.7 | async-start | bytes 1048576 | tf_op jit(solution)/shard_map/psum | solution.py:17
  1008.4 280.6 %all-reduce.23.cloned.1.call-start = ((), (), s32[]{:S(2)}) async-start(), calls=%async_computation.8 | async-start | bytes 1048576 | tf_op jit(solution)/shard_map/psum | solution.py:17
Sparse Core Ops, SparseCore 0:
  9.1 66.0 all-gather.8
  78.3 71.8 all-gather.4
  152.8 75.1 all-reduce.10
  231.5 36.4 all-gather.6
  298.6 141.7 all-reduce.12
  516.4 126.4 all-reduce.14
  645.5 151.2 all-reduce.16
  799.9 142.7 all-reduce.18
  1008.5 126.5 all-reduce.20
  1137.7 151.2 all-reduce.22
where the time goes:
time: 1300 us
  waiting for transfers between devices  1100 us (85%)
  other arithmetic  120 us (9%)
  matrix products  25.1 us (2%)
  local copies, waits for them, and re-layouts  20.8 us (2%)
  between operations  18.1 us (1%)
    psum x7, waiting for transfers between devices, broadcast(): return lax.psum(jnp.where(mine, x, jnp.zeros_like(x)), axis)  919 us
    all_gather x1, waiting for transfers between devices, local(): panel_rows = lax.all_gather(panel_block, 'col', axis=1, tiled=True)  71.9 us
    another operation x13, other arithmetic, factor_pivot(): lower_pivot = jnp.linalg.cholesky(safe_block)  68.6 us
    all_gather x1, waiting for transfers between devices, local(): lax.all_gather(coupling_local, 'col', axis=1, tiled=True)  67.9 us
    another operation x5, other arithmetic, factor_pivot(): jax.scipy.linalg.solve_triangular(lower_pivot, identity, lower=True)  39.4 us
    all_gather x1, waiting for transfers between devices, local(): column_slab = lax.all_gather(schur_part, 'row', axis=0, tiled=True)  32.6 us
  transfers between devices with their start and end apart: 11, of which 11 were waited for; matrix products, arithmetic and copies ran while one was open for 0% of the time, Pallas kernels for 0%

commit v1 on v0

v1 whole, which is shorter than its diff:
```python
import jax
import jax.numpy as jnp
from jax import lax
from jax.experimental import pallas as pl
from jax.experimental.pallas import tpu as pltpu
from jax.sharding import PartitionSpec as P

f32 = jnp.float32
bf16 = jnp.bfloat16
MESH = pl.DeviceIdType.MESH
NT = (((1,), (1,)), ((), ()))
NN = (((1,), (0,)), ((), ()))
TN = (((0,), (0,)), ((), ()))


def rcopy(src, dst, send, recv, dev):
    return pltpu.make_async_remote_copy(
        src_ref=src, dst_ref=dst, send_sem=send, recv_sem=recv, device_id=dev, device_id_type=MESH
    )


class Ring:
    def __init__(self, buf, send, recv, s, r, xlo, z):
        self.right, self.left = [], []
        to_right = (s, r, xlo * 8 + lax.rem(z + 1, 8))
        to_left = (s, r, xlo * 8 + lax.rem(z + 7, 8))
        for t in range(4):
            slot = buf.at[lax.rem(z - t + 8, 8)]
            self.right.append(rcopy(slot, slot, send.at[t], recv.at[t], to_right))
        for t in range(3):
            slot = buf.at[lax.rem(z + t, 8)]
            self.left.append(rcopy(slot, slot, send.at[4 + t], recv.at[4 + t], to_left))

    def start(self, t):
        self.right[t].start()
        if t < 3:
            self.left[t].start()

    def arrive(self, t):
        self.right[t].wait_recv()
        if t < 3:
            self.left[t].wait_recv()

    def drain(self):
        for copy in self.right + self.left:
            copy.wait_send()


class Column:
    def __init__(self, buf, send, recv, s, r, c):
        core = lax.rem(r, 2)
        h = 4 * s + r // 2
        own = buf.at[8 * s + r]
        partner = (s, r + 1 - 2 * core, c)
        self.out, self.share = [], [rcopy(own, own, send.at[7], recv.at[7], partner)]
        for d in range(1, 8):
            to = lax.rem(h + d, 8)
            dev = (to // 4, 2 * lax.rem(to, 4) + core, c)
            self.out.append(rcopy(own, own, send.at[d - 1], recv.at[d - 1], dev))
            slot = buf.at[2 * lax.rem(h - d + 8, 8) + core]
            self.share.append(rcopy(slot, slot, send.at[7 + d], recv.at[7 + d], partner))

    def start(self):
        for copy in self.out:
            copy.start()
        self.share[0].start()

    def forward(self, d):
        self.out[d - 1].wait_recv()
        self.share[d].start()

    def finish(self):
        for copy in self.share:
            copy.wait_recv()

    def drain(self):
        for copy in self.out + self.share:
            copy.wait_send()


def gather_kernel(
    map_ref, pat_ref, upd_ref, cpl_ref, inv_ref, front_ref,
    a_ref, ag_ref, col_ref,
    invbuf, cbuf, ptile, prow, pcol, ubuf, f00, a00,
    loc_sem, x_send, x_recv, u_send, u_recv,
    c_send, c_recv, p_send, p_recv, f_send, f_recv, g_send, g_recv,
    pr_send, pr_recv, pc_send, pc_recv, k1_send, k1_recv, k2_send, k2_recv,
    fs_send, fs_recv, cs_send, cs_recv, as_send, as_recv,
):
    s, r, c = lax.axis_index("sub"), lax.axis_index("row"), lax.axis_index("col")
    xlo, z = c // 8, lax.rem(c, 8)
    group = 8 * s + r
    lead = group == 0
    root = jnp.logical_and(lead, c == 0)
    xpart = (s, r, lax.rem(c + 8, 16))

    inv_loc = pltpu.make_async_copy(inv_ref.at[0], invbuf.at[xlo], loc_sem.at[0])
    inv_rem = rcopy(inv_ref.at[0], invbuf.at[xlo], x_send.at[0], x_recv.at[0], xpart)
    mine = pl.ds(pl.multiple_of(xlo * 256, 256), 256)
    theirs = pl.ds(pl.multiple_of(256 - xlo * 256, 256), 256)
    cpl_loc = pltpu.make_async_copy(cpl_ref.at[0, mine], cbuf.at[z, xlo], loc_sem.at[1])
    cpl_rem = rcopy(cpl_ref.at[0, theirs], cbuf.at[z, xlo], x_send.at[1], x_recv.at[1], xpart)
    cpl_rem.start()
    cpl_loc.start()
    inv_loc.start()
    inv_rem.start()
    u_copies = []
    for i in range(2):
        block = 2 * r + i
        dest = (block // 8, lax.rem(block, 8), c)
        src = upd_ref.at[0, pl.ds(256 * i, 256)]
        rem = rcopy(src, ubuf.at[s], u_send.at[i], u_recv.at[s], dest)
        loc = pltpu.make_async_copy(src, ubuf.at[s], u_recv.at[s])
        own = jnp.logical_and(block // 8 == s, lax.rem(block, 8) == r)
        u_copies.append((own, rem))

        @pl.when(own)
        def _():
            loc.start()

        @pl.when(jnp.logical_not(own))
        def _():
            rem.start()

    cpl_loc.wait()
    cpl_rem.wait_recv()
    ring_c = Ring(cbuf, c_send, c_recv, s, r, xlo, z)
    ring_c.start(0)

    def weight(child, i, k):
        ro = map_ref[child, group] - 2 * group
        co = map_ref[child, c] - 2 * c
        return (ro == i).astype(f32) * (co == k).astype(f32)

    for child in range(2):
        rcopy(ubuf.at[child], ubuf.at[child], u_send.at[0], u_recv.at[child], xpart).wait_recv()
    for i in range(2):
        for k in range(2):
            at = (slice(256 * i, 256 * i + 256), slice(256 * k, 256 * k + 256))
            value = front_ref[at] * pat_ref[i, k].astype(f32)
            for child in range(2):
                value = value + weight(child, i, k) * ubuf[child]
            a_ref[at] = value

    fs_copies = []
    for cp in range(16):
        piece = a_ref.at[pl.ds(64 * (cp % 8), 64)]
        fs_copies.append(rcopy(piece, f00.at[cp % 8], fs_send.at[cp], fs_recv.at[0], (0, 0, cp)))

    @pl.when(root)
    def _():
        pltpu.make_async_copy(a_ref.at[pl.ds(0, 64)], f00.at[0], fs_recv.at[0]).start()
        for copy in fs_copies[1:]:
            copy.start()

    for t in range(1, 4):
        ring_c.arrive(t - 1)
        ring_c.start(t)
    ring_f = Ring(f00, f_send, f_recv, s, r, xlo, z)

    @pl.when(lead)
    def _():
        rcopy(f00.at[0], f00.at[0], fs_send.at[0], fs_recv.at[0], xpart).wait_recv()
        ring_f.start(0)

    inv_loc.wait()
    inv_rem.wait_recv()
    ring_c.arrive(3)

    for half in range(2):
        total = jnp.zeros((256, 128), f32)
        for kz in range(8):
            for kh in range(2):
                total = total + lax.dot_general(
                    cbuf[kz, kh],
                    invbuf[half, :, (kh * 8 + kz) * 128 : (kh * 8 + kz + 1) * 128],
                    NT,
                    preferred_element_type=f32,
                )
        ptile[:, 128 * half : 128 * half + 128] = total.astype(bf16)

    block = 2 * r + xlo
    pr_copies = []
    for xh in range(2):
        dest = (block // 8, lax.rem(block, 8), xh * 8 + z)
        rem = rcopy(ptile, prow.at[z, s], pr_send.at[xh], pr_recv.at[s], dest)
        loc = pltpu.make_async_copy(ptile, prow.at[z, s], pr_recv.at[s])
        own = jnp.logical_and(
            jnp.logical_and(block // 8 == s, lax.rem(block, 8) == r), xlo == xh
        )
        pr_copies.append((own, rem))

        @pl.when(own)
        def _():
            loc.start()

        @pl.when(jnp.logical_not(own))
        def _():
            rem.start()

    pc_slot = pcol.at[2 * z + s]
    pc_rem = rcopy(
        ptile, pc_slot, pc_send.at[0], pc_recv.at[0], (z // 4, 2 * lax.rem(z, 4) + s, block)
    )
    pc_loc = pltpu.make_async_copy(ptile, pc_slot, pc_recv.at[0])
    pc_own = jnp.logical_and(
        jnp.logical_and(z // 4 == s, 2 * lax.rem(z, 4) + s == r), block == c
    )

    @pl.when(pc_own)
    def _():
        pc_loc.start()

    @pl.when(jnp.logical_not(pc_own))
    def _():
        pc_rem.start()

    for child in range(2):
        slot = prow.at[z, child]
        rcopy(slot, slot, pr_send.at[0], pr_recv.at[child], xpart).wait_recv()
    ring_p = Ring(prow, p_send, p_recv, s, r, xlo, z)
    ring_p.start(0)
    rcopy(pcol.at[group], pcol.at[group], pc_send.at[0], pc_recv.at[0], xpart).wait_recv()
    col_p = Column(pcol, k1_send, k1_recv, s, r, c)
    col_p.start()
    for t in range(1, 4):
        ring_p.arrive(t - 1)
        ring_p.start(t)

        @pl.when(lead)
        def _():
            ring_f.arrive(t - 1)
            ring_f.start(t)

        col_p.forward(2 * t - 1)
        col_p.forward(2 * t)
    col_p.forward(7)
    ring_p.arrive(3)
    col_p.finish()

    def product(child, columns):
        total = jnp.zeros((256, 256), f32)
        for kz in range(8):
            total = total + lax.dot_general(
                prow[kz, child], columns(kz, child), NT, preferred_element_type=f32
            )
        return total

    @pl.when(root)
    def _():
        for copy in fs_copies[1:]:
            copy.wait_send()

    schur = [product(child, lambda kz, ch: pcol[2 * kz + ch]) for child in range(2)]
    for i in range(2):
        for k in range(2):
            at = (slice(256 * i, 256 * i + 256), slice(256 * k, 256 * k + 256))
            a_ref[at] = a_ref[at] - weight(0, i, k) * schur[0] - weight(1, i, k) * schur[1]

    as_copies, cs_copies = [], []
    for cp in range(16):
        as_copies.append(
            rcopy(
                a_ref.at[pl.ds(64 * (cp % 8), 64)], ag_ref.at[cp % 8],
                as_send.at[cp], as_recv.at[0], (c // 8, lax.rem(c, 8), cp),
            )
        )
        source = a_ref if cp % 2 else a00
        cs_copies.append(
            rcopy(
                source.at[pl.ds(64 * (cp // 2), 64)], col_ref.at[cp],
                cs_send.at[cp], cs_recv.at[0], (cp // 8, cp % 8, c),
            )
        )

    @pl.when(lead)
    def _():
        ring_f.arrive(3)
        ring_f.drain()
        lead_prod = [product(child, lambda kz, ch: prow[kz, ch]) for child in range(2)]
        for i in range(2):
            for k in range(2):
                for q in range(4):
                    value = f00[4 * i + q, :, 256 * k : 256 * k + 256]
                    for child in range(2):
                        off = map_ref[child, 0]
                        w = (off == i).astype(f32) * (off == k).astype(f32)
                        value = value - w * lead_prod[child][64 * q : 64 * q + 64]
                    a00[256 * i + 64 * q : 256 * i + 64 * q + 64, 256 * k : 256 * k + 256] = value
        pltpu.make_async_copy(a00.at[pl.ds(0, 64)], col_ref.at[0], cs_recv.at[0]).start()
        for copy in cs_copies[1:]:
            copy.start()

        @pl.when(c == 0)
        def _():
            pltpu.make_async_copy(a_ref.at[pl.ds(0, 64)], ag_ref.at[0], as_recv.at[0]).start()

        @pl.when(c != 0)
        def _():
            as_copies[0].start()

        for copy in as_copies[1:]:
            copy.start()

    rcopy(col_ref.at[group], col_ref.at[group], cs_send.at[0], cs_recv.at[0], xpart).wait_recv()
    col_a = Column(col_ref, k2_send, k2_recv, s, r, c)
    col_a.start()
    rcopy(ag_ref.at[z], ag_ref.at[z], as_send.at[0], as_recv.at[0], xpart).wait_recv()
    ring_g = Ring(ag_ref, g_send, g_recv, s, r, xlo, z)
    ring_g.start(0)
    for t in range(1, 4):
        ring_g.arrive(t - 1)
        ring_g.start(t)
        col_a.forward(2 * t - 1)
        col_a.forward(2 * t)
    col_a.forward(7)
    ring_g.arrive(3)
    col_a.finish()

    @pl.when(lead)
    def _():
        for copy in cs_copies[1:] + as_copies[1:]:
            copy.wait_send()

        @pl.when(c != 0)
        def _():
            as_copies[0].wait_send()

    for own, rem in u_copies + pr_copies + [(pc_own, pc_rem)]:
        @pl.when(jnp.logical_not(own))
        def _():
            rem.wait_send()

    cpl_rem.wait_send()
    inv_rem.wait_send()
    for ring in (ring_c, ring_p, ring_g, col_p, col_a):
        ring.drain()


def gather_call(child_map, pattern, update, coupling, inverse, front):
    vmem = pl.BlockSpec(memory_space=pltpu.VMEM)
    smem = pl.BlockSpec(memory_space=pltpu.SMEM)
    dma = pltpu.SemaphoreType.DMA
    ring = [dma((7,)), dma((7,))]
    column = [dma((15,)), dma((15,))]
    return pl.pallas_call(
        gather_kernel,
        out_shape=[
            jax.ShapeDtypeStruct((512, 512), f32),
            jax.ShapeDtypeStruct((8, 64, 512), f32),
            jax.ShapeDtypeStruct((16, 64, 512), f32),
        ],
        in_specs=[smem, smem, vmem, vmem, vmem, vmem],
        out_specs=[vmem, vmem, vmem],
        scratch_shapes=[
            pltpu.VMEM((2, 128, 2048), bf16),
            pltpu.VMEM((8, 2, 256, 128), bf16),
            pltpu.VMEM((256, 256), bf16),
            pltpu.VMEM((8, 2, 256, 256), bf16),
            pltpu.VMEM((16, 256, 256), bf16),
            pltpu.VMEM((2, 256, 256), f32),
            pltpu.VMEM((8, 64, 512), f32),
            pltpu.VMEM((512, 512), f32),
            dma((2,)), dma((2,)), dma((2,)), dma((2,)), dma((2,)),
            *ring, *ring, *ring, *ring,
            dma((2,)), dma((2,)), dma((1,)), dma((1,)),
            *column, *column,
            dma((16,)), dma((1,)), dma((16,)), dma((1,)), dma((16,)), dma((1,)),
        ],
        compiler_params=pltpu.CompilerParams(
            has_side_effects=True, vmem_limit_bytes=48 * 1024 * 1024
        ),
        cost_estimate=pl.CostEstimate(flops=800_000_000, bytes_accessed=8_000_000, transcendentals=0),
    )(child_map, pattern, update, coupling, inverse, front)


def lanes(x, k):
    return jnp.broadcast_to(x[:, k : k + 1], (8, 128))


def rows(x, k):
    return jnp.broadcast_to(x[k : k + 1, :], (8, 128))


def pivot_block(d):
    left = [d[8 * i : 8 * i + 8, :] for i in range(16)]
    rid = lax.broadcasted_iota(jnp.int32, (8, 128), 0)
    cid = lax.broadcasted_iota(jnp.int32, (8, 128), 1)
    right = [(cid == rid + 8 * i).astype(f32) for i in range(16)]
    for b in range(16):
        lead = [lanes(left[b], 8 * b + k) for k in range(8)]
        lo, ro = left[b], right[b]
        top, inv, row_l, row_r = {}, [], [], []
        for k in range(8):
            rinv = lax.rsqrt(rows(lead[k], k))
            f = jnp.where(rid > k, lead[k] * rinv, 0.0)
            for m in range(k + 1, 8):
                top[k, m] = rows(lead[m], k) * rinv
                lead[m] = lead[m] - f * top[k, m]
            row_l.append(rows(lo, k) * rinv)
            row_r.append(rows(ro, k) * rinv)
            lo = lo - f * row_l[k]
            ro = ro - f * row_r[k]
            inv.append(rinv)
        left[b], right[b] = row_l[0], row_r[0]
        for k in range(1, 8):
            left[b] = jnp.where(rid == k, row_l[k], left[b])
            right[b] = jnp.where(rid == k, row_r[k], right[b])
        for i in range(b + 1, 16):
            own = [lanes(left[i], 8 * b + k) for k in range(8)]
            lo, ro = left[i], right[i]
            for k in range(8):
                f = own[k] * inv[k]
                for m in range(k + 1, 8):
                    own[m] = own[m] - f * top[k, m]
                lo = lo - f * row_l[k]
                ro = ro - f * row_r[k]
            left[i], right[i] = lo, ro
    return left, right


def hdot(a, b, dims):
    return lax.dot_general(a, b, dims, precision=lax.Precision.HIGHEST, preferred_element_type=f32)


def factor_kernel(a_ref, ag_ref, col_ref, o_ref, lead, both, ut, vt):
    s, r, c = lax.axis_index("sub"), lax.axis_index("row"), lax.axis_index("col")
    group = 8 * s + r
    for h in range(8):
        lead[64 * h : 64 * h + 64, :] = col_ref[2 * h]
        both[64 * h : 64 * h + 64, 0:512] = ag_ref[h]
        both[64 * h : 64 * h + 64, 512:1024] = col_ref[2 * h + 1]

    @pl.loop(0, 4)
    def _(kb):
        at = pl.ds(pl.multiple_of(kb * 128, 128), 128)
        left, right = pivot_block(lead[at, at])
        for i in range(16):
            ut[8 * i : 8 * i + 8, :] = left[i]
            vt[8 * i : 8 * i + 8, :] = right[i]
        row_id = lax.broadcasted_iota(jnp.int32, (512, 128), 0)
        panel = hdot(lead[:, at], vt[...], NT)
        panel = jnp.where(row_id >= (kb + 1) * 128, panel, 0.0)
        lead[...] = lead[...] - hdot(panel, panel, NT)
        done = hdot(vt[...], both[at, :], NN)
        both[...] = both[...] - hdot(panel, done, NN)
        both[at, :] = done
        lead[:, at] = panel
        lead[at, at] = ut[...].T

    row_id = lax.broadcasted_iota(jnp.int32, (512, 512), 0)
    col_id = lax.broadcasted_iota(jnp.int32, (512, 512), 1)

    @pl.when(group == 0)
    def _():
        keep = jnp.logical_and(c == 0, col_id <= row_id)
        o_ref[...] = jnp.where(keep, lead[...], 0.0)

    @pl.when(jnp.logical_and(group != 0, c == 0))
    def _():
        o_ref[...] = both[:, 0:512].T

    @pl.when(jnp.logical_and(group != 0, c != 0))
    def _():
        o_ref[...] = a_ref[...] - hdot(both[:, 0:512], both[:, 512:1024], TN)


def factor_call(tile, row_part, col_part):
    vmem = pl.BlockSpec(memory_space=pltpu.VMEM)
    return pl.pallas_call(
        factor_kernel,
        out_shape=jax.ShapeDtypeStruct((512, 512), f32),
        in_specs=[vmem, vmem, vmem],
        out_specs=vmem,
        scratch_shapes=[
            pltpu.VMEM((512, 512), f32),
            pltpu.VMEM((512, 1024), f32),
            pltpu.VMEM((128, 128), f32),
            pltpu.VMEM((128, 128), f32),
        ],
        compiler_params=pltpu.CompilerParams(vmem_limit_bytes=48 * 1024 * 1024),
        cost_estimate=pl.CostEstimate(flops=5_000_000_000, bytes_accessed=5_000_000, transcendentals=512),
    )(tile, row_part, col_part)


def local(child_update, child_coupling, pivot_inverse, child_map, parent_front, block_pattern):
    tile, row_part, col_part = gather_call(
        child_map, block_pattern, child_update, child_coupling, pivot_inverse, parent_front
    )
    return factor_call(tile, row_part, col_part)


def solution(mesh):
    return jax.shard_map(
        local,
        mesh=mesh,
        in_specs=(
            P("sub", "row", "col"),
            P("sub", "row", "col"),
            P("sub", "col", None),
            P(),
            P(("sub", "row"), "col"),
            P(("sub", "row"), "col"),
        ),
        out_specs=P(("sub", "row"), "col"),
        check_vma=False,
    )
```

time: 1300 us -> 207 us (0.16)
  waiting for transfers between devices: 1100 us -> 0 us
  Pallas kernels: 0 us -> 197 us
  other arithmetic: 120 us -> 0 us
  matrix products: 25.1 us -> 0 us
  between operations: 18.1 us -> 0.02 us
  local copies, waits for them, and re-layouts: 20.8 us -> 7.15 us
    psum x7 -> x0, waiting for transfers between devices: 919 us -> none  [broadcast(): return lax.psum(jnp.where(mine, x, jnp.zeros_like(x)), axis)]
    pallas_call x0 -> x2, Pallas kernels: none -> 197 us  [the longest x1 164 us: gather_call(): pl.pallas_call(gather_kernel, out_shape=[jax.ShapeDtypeStruct((512, 512),...]
    all_gather x3 -> x0, waiting for transfers between devices: 172 us -> none  [the longest x1 71.9 us: local(): panel_rows = lax.all_gather(panel_block, 'col', axis=1, tiled=True)]
    another operation x20 -> x0, other arithmetic: 108 us -> none  [the longest x13 68.6 us: factor_pivot(): lower_pivot = jnp.linalg.cholesky(safe_block)]
    dot_general x8 -> x0, matrix products: 21.9 us -> none  [the longest x2 7.54 us: select_rows(): return jnp.einsum('ib,bxy->ixy', onehot, child_blocks, precision=highest)]
  transfers between devices with their start and end apart: 11 -> 0, of which waited for: 11 -> 0; matrix products, arithmetic and copies ran while one was open for 0% -> 0% of each run, Pallas kernels for 0% -> 0%
where the time goes in v1:
time: 207 us; the launch traced here: 204 us
  Pallas kernels  197 us (95%)
  local copies, waits for them, and re-layouts  7.15 us (3%)
    pallas_call x1, Pallas kernels, gather_call(): pl.pallas_call(gather_kernel, out_shape=[jax.ShapeDtypeStruct((512, 512),...  164 us
    pallas_call x1, Pallas kernels, factor_call(): pl.pallas_call(factor_kernel, out_shape=jax.ShapeDtypeStruct((512, 512),...  33.2 us
    unnamed x14, local copies, waits for them, and re-layouts  7.15 us

profile of v1, /device:TPU:1, one launch (start us, length us, event | category | flops | bytes accessed | tf_op | source)
XLA Modules:
  0.0 204.0 jit_solution(16061216051048430898)
XLA Ops:
  0.0 0.0 copy-start
  0.0 1.2 copy-done
  1.2 0.0 copy-start.1
  1.2 1.0 copy-done.1
  2.3 0.0 copy-start.2
  2.3 1.0 copy-done.2
  3.3 0.0 copy-start.3
  3.3 0.9 copy-done.3
  4.2 0.0 copy-start.4
  4.2 0.7 copy-done.4
  4.9 0.0 copy-start.5
  4.9 0.7 copy-done.5
  5.6 163.7 %shard_map.64 = (f32[512,512]{1,0:T(8,128)S(1)}, f32[8,64,512]{2,1,0:T(8,128)S(1)}, f32[16,64,512]{2,1,0:T(8,128)}) custom-call(s32[2,16]{1,0:T(2,128)S(1)} %copy-done.4, s32[2,2]{1,0:T(2,128)S(1)} %copy-done.5, f32[1,512,256]{2,1,0:T(8,128)S(1)} %copy-done.1, bf16[1,512,128]{2,1,0:T(8,128)(2,1)S(1)} %copy-done.3, bf16[1,128,2048]{2,1,0:T(8,128)(2,1)S(1)} %copy-done.2, ...), custom_call_target="tpu_custom_call" | custom-call | flops 800000000 | bytes 8000000 | tf_op jit(solution)/shard_map/pallas_call | solution.py:346
  169.2 0.0 copy-start.6
  169.2 1.6 copy-done.6
  170.8 33.2 %shard_map.65 = f32[512,512]{1,0:T(8,128)} custom-call(f32[512,512]{1,0:T(8,128)S(1)} %get-tuple-element.8.a_ref, f32[8,64,512]{2,1,0:T(8,128)S(1)} %get-tuple-element.9.ag_ref, f32[16,64,512]{2,1,0:T(8,128)S(1)} %copy-done.6), custom_call_target="tpu_custom_call" | custom-call | flops 5000000000 | bytes 5000000 | tf_op jit(solution)/shard_map/pallas_call | solution.py:470
Async XLA Ops:
  0.0 1.2 copy-start
  1.2 1.0 copy-start.1
  2.3 1.0 copy-start.2
  3.3 0.9 copy-start.3
  4.2 0.7 copy-start.4
  4.9 0.7 copy-start.5
  169.2 1.6 copy-start.6

commit v2 on v0

v2 whole, which is shorter than its diff:
```python
import jax
import jax.numpy as jnp
from jax import lax
from jax.experimental import pallas as pl
from jax.experimental.pallas import tpu as pltpu
from jax.sharding import PartitionSpec as P

f32 = jnp.float32
bf16 = jnp.bfloat16
MESH = pl.DeviceIdType.MESH
NT = (((1,), (1,)), ((), ()))
NN = (((1,), (0,)), ((), ()))
TN = (((0,), (0,)), ((), ()))


def rcopy(src, dst, send, recv, dev):
    return pltpu.make_async_remote_copy(
        src_ref=src, dst_ref=dst, send_sem=send, recv_sem=recv, device_id=dev, device_id_type=MESH
    )


def aligned(start, size):
    return pl.ds(pl.multiple_of(start, size), size)


class Ring:
    def __init__(self, buf, send, recv, s, r, xlo, z):
        self.buf, self.send, self.recv, self.z = buf, send, recv, z
        self.to_right = (s, r, xlo * 8 + lax.rem(z + 1, 8))
        self.to_left = (s, r, xlo * 8 + lax.rem(z + 7, 8))

    def right(self, t):
        slot = self.buf.at[lax.rem(self.z - t + 8, 8)]
        return rcopy(slot, slot, self.send.at[t], self.recv.at[t], self.to_right)

    def left(self, t):
        slot = self.buf.at[lax.rem(self.z + t, 8)]
        return rcopy(slot, slot, self.send.at[4 + t], self.recv.at[4 + t], self.to_left)

    def both(self, t, act):
        act(self.right(t))
        if isinstance(t, int):
            if t < 3:
                act(self.left(t))
        else:

            @pl.when(t < 3)
            def _():
                act(self.left(t))

    def start(self, t):
        self.both(t, lambda copy: copy.start())

    def arrive(self, t):
        self.both(t, lambda copy: copy.wait_recv())

    def drain(self):
        for t in range(4):
            self.both(t, lambda copy: copy.wait_send())


class Spread:
    def __init__(self, slot, send, recv, n, chip, core, device, partner):
        self.slot, self.send, self.recv, self.n = slot, send, recv, n
        self.chip, self.core, self.device, self.partner = chip, core, device, partner

    def out(self, d):
        own = self.slot(2 * self.chip + self.core)
        to = lax.rem(self.chip + d, self.n)
        return rcopy(own, own, self.send.at[d], self.recv.at[d], self.device(to))

    def share(self, d):
        slot = self.slot(2 * lax.rem(self.chip - d + self.n, self.n) + self.core)
        return rcopy(slot, slot, self.send.at[self.n + d], self.recv.at[self.n + d], self.partner)

    def start(self):
        for d in range(1, self.n):
            self.out(d).start()
        self.share(0).start()

    def forward(self, d):
        self.out(d).wait_recv()
        self.share(d).start()

    def finish(self):
        for d in range(self.n):
            self.share(d).wait_recv()

    def drain(self):
        for d in range(1, self.n):
            self.out(d).wait_send()
        for d in range(self.n):
            self.share(d).wait_send()


def lanes(x, k):
    return jnp.broadcast_to(x[:, k : k + 1], (8, 128))


def rows(x, k):
    return jnp.broadcast_to(x[k : k + 1, :], (8, 128))


def pivot_block(d):
    left = [d[8 * i : 8 * i + 8, :] for i in range(16)]
    rid = lax.broadcasted_iota(jnp.int32, (8, 128), 0)
    cid = lax.broadcasted_iota(jnp.int32, (8, 128), 1)
    right = [(cid == rid + 8 * i).astype(f32) for i in range(16)]
    for b in range(16):
        lead = [lanes(left[b], 8 * b + k) for k in range(8)]
        lo, ro = left[b], right[b]
        top, inv, row_l, row_r = {}, [], [], []
        for k in range(8):
            rinv = lax.rsqrt(rows(lead[k], k))
            f = jnp.where(rid > k, lead[k] * rinv, 0.0)
            for m in range(k + 1, 8):
                top[k, m] = rows(lead[m], k) * rinv
                lead[m] = lead[m] - f * top[k, m]
            row_l.append(rows(lo, k) * rinv)
            row_r.append(rows(ro, k) * rinv)
            lo = lo - f * row_l[k]
            ro = ro - f * row_r[k]
            inv.append(rinv)
        left[b], right[b] = row_l[0], row_r[0]
        for k in range(1, 8):
            left[b] = jnp.where(rid == k, row_l[k], left[b])
            right[b] = jnp.where(rid == k, row_r[k], right[b])
        for i in range(b + 1, 16):
            own = [lanes(left[i], 8 * b + k) for k in range(8)]
            lo, ro = left[i], right[i]
            for k in range(8):
                f = own[k] * inv[k]
                for m in range(k + 1, 8):
                    own[m] = own[m] - f * top[k, m]
                lo = lo - f * row_l[k]
                ro = ro - f * row_r[k]
            left[i], right[i] = lo, ro
    return left, right


def hdot(a, b, dims):
    return lax.dot_general(a, b, dims, precision=lax.Precision.HIGHEST, preferred_element_type=f32)


def kernel(
    map_ref, pat_ref, upd_ref, cpl_ref, inv_ref, front_ref, o_ref,
    invbuf, cbuf, ptile, prow, pcol, ubuf, front, tile, fsrc, fbuf, gbuf,
    fc, p0, tbuf, lead, both, ut, vt,
    loc_sem, fa_send, fa_recv, fb_send, fb_recv, d1_send, d1_recv, d2_send, d2_recv,
    t_send, t_recv, x_send, x_recv, u_send, u_recv, c_send, c_recv, p_send, p_recv,
    g_send, g_recv, pr_send, pr_recv, pc_send, pc_recv, k1_send, k1_recv, kf_send, kf_recv,
    rs_send, rs_recv, rp_send, rp_recv, gs_send, gs_recv, cs_send, cs_recv, e_send, e_recv,
):
    s, r, c = lax.axis_index("sub"), lax.axis_index("row"), lax.axis_index("col")
    xlo, z = c // 8, lax.rem(c, 8)
    y, core = r // 2, lax.rem(r, 2)
    group = 8 * s + r
    chip = 4 * s + y
    leads = group == 0
    root = jnp.logical_and(leads, c == 0)
    block = 2 * r + xlo
    xpart = (s, r, lax.rem(c + 8, 16))
    cpart = (s, r + 1 - 2 * core, c)
    hpart = (1 - s, r, c)

    def at_group(g):
        return (g // 8, lax.rem(g, 8), c)

    inv_loc = pltpu.make_async_copy(inv_ref.at[0], invbuf.at[xlo], loc_sem.at[0])
    mine, theirs = aligned(xlo * 256, 256), aligned(256 - xlo * 256, 256)
    cpl_loc = pltpu.make_async_copy(cpl_ref.at[0, mine], cbuf.at[z, xlo], loc_sem.at[1])
    front_loc = pltpu.make_async_copy(front_ref, front, loc_sem.at[2])
    inv_loc.start()
    cpl_loc.start()
    front_loc.start()

    barrier = pltpu.get_barrier_semaphore()

    def same(dev):
        return jnp.logical_and(jnp.logical_and(dev[0] == s, dev[1] == r), dev[2] == c)

    def hello(dev):
        pl.semaphore_signal(barrier, inc=1, device_id=dev, device_id_type=MESH)

    def hello_other(dev):
        @pl.when(jnp.logical_not(same(dev)))
        def _():
            hello(dev)

    for d in range(1, 16):
        hello((s, r, lax.rem(c + d, 16)))
        hello(at_group(lax.rem(group + d, 16)))
    half_block = group // 2
    for child in range(2):
        hello_other((child, half_block, lax.rem(group, 2) * 8 + z))
    hello_other((core, c // 2, lax.rem(c, 2) * 8 + chip))
    hello_other((0, 0, group))
    pr_dest = [(block // 8, lax.rem(block, 8), xh * 8 + z) for xh in range(2)]
    pc_dest = (z // 4, 2 * lax.rem(z, 4) + s, block)

    def other(dev):
        return jnp.where(same(dev), 0, 1)

    expected = 30 + other(pr_dest[0]) + other(pr_dest[1]) + other(pc_dest)
    expected = expected + jnp.where(leads, 16 - jnp.where(c == 0, 1, 0), 0)
    pl.semaphore_wait(barrier, expected)

    fa_copies = [
        rcopy(cpl_ref.at[0, pl.ds(32 * q, 32)], fc.at[c], fa_send.at[q], fa_recv.at[0], (s, q, c))
        for q in range(1, 8)
    ]
    u_copies = []
    for i in range(2):
        dest = at_group(2 * r + i)
        u_copies.append((same(dest), rcopy(
            upd_ref.at[0, pl.ds(256 * i, 256)], ubuf.at[s], u_send.at[i], u_recv.at[s], dest
        ), i))

    def u_start(entry):
        own, rem, i = entry

        @pl.when(own)
        def _():
            pltpu.make_async_copy(
                upd_ref.at[0, pl.ds(256 * i, 256)], ubuf.at[s], u_recv.at[s]
            ).start()

        @pl.when(jnp.logical_not(own))
        def _():
            rem.start()

    @pl.when(r == 0)
    def _():
        for copy in fa_copies:
            copy.start()
        pltpu.make_async_copy(cpl_ref.at[0, pl.ds(0, 32)], fc.at[c], fa_recv.at[0]).start()
        u_start(u_copies[0])

    cpl_rem = rcopy(cpl_ref.at[0, theirs], cbuf.at[z, xlo], x_send.at[1], x_recv.at[1], xpart)
    cpl_rem.start()
    inv_half = aligned(64 * core, 64)
    inv_rem = rcopy(
        inv_ref.at[0, inv_half], invbuf.at[xlo, inv_half], x_send.at[0], x_recv.at[0], xpart
    )
    inv_rem.start()

    rcopy(fc.at[c], fc.at[c], fa_send.at[0], fa_recv.at[0], xpart).wait_recv()
    fb_copies = [
        rcopy(fc.at[c], fc.at[c], fb_send.at[d], fb_recv.at[d], (s, r, lax.rem(c + d, 16)))
        for d in range(1, 16)
    ]
    for copy in fb_copies:
        copy.start()

    cpl_loc.wait()
    cpl_rem.wait_recv()
    ring_c = Ring(cbuf, c_send, c_recv, s, r, xlo, z)
    ring_c.start(0)

    def weight(child, i, k):
        ro = map_ref[child, group] - 2 * group
        co = map_ref[child, c] - 2 * c
        return (ro == i).astype(f32) * (co == k).astype(f32)

    def quarter(i, k):
        return (slice(256 * i, 256 * i + 256), slice(256 * k, 256 * k + 256))

    def own_entries():
        for child in range(2):
            slot = ubuf.at[child]
            rcopy(slot, slot, u_send.at[0], u_recv.at[child], xpart).wait_recv()
        for i in range(2):
            for k in range(2):
                value = front[quarter(i, k)] * pat_ref[i, k].astype(f32)
                for child in range(2):
                    value = value + weight(child, i, k) * ubuf[child]
                tile[quarter(i, k)] = value

    front_loc.wait()
    gs_copies, cs_copies, rs_copies = [], [], []
    for cp in range(16):
        gs_copies.append(rcopy(
            fsrc.at[pl.ds(64 * (cp % 8), 64)], gbuf.at[cp % 8],
            gs_send.at[cp], gs_recv.at[0], (c // 8, lax.rem(c, 8), cp),
        ))
        piece = fsrc.at[pl.ds(32 * cp, 32)]
        cs_copies.append(rcopy(
            piece, fbuf.at[cp, 1], cs_send.at[cp], cs_recv.at[0], (cp // 8, cp % 8, c)
        ))
        rs_copies.append(rcopy(
            piece, fbuf.at[cp, 0], rs_send.at[cp], rs_recv.at[0], (cp // 8, cp % 8, 0)
        ))

    @pl.when(leads)
    def _():
        own_entries()
        fsrc[...] = tile[...].astype(bf16)

        @pl.when(c == 0)
        def _():
            for copy in rs_copies[1:]:
                copy.start()
            pltpu.make_async_copy(fsrc.at[pl.ds(0, 32)], fbuf.at[0, 0], rs_recv.at[0]).start()
            pltpu.make_async_copy(fsrc.at[pl.ds(0, 64)], gbuf.at[0], gs_recv.at[0]).start()

        pltpu.make_async_copy(fsrc.at[pl.ds(0, 32)], fbuf.at[0, 1], cs_recv.at[0]).start()
        for copy in cs_copies[1:]:
            copy.start()

        @pl.when(c != 0)
        def _():
            gs_copies[0].start()

        for copy in gs_copies[1:]:
            copy.start()

    for copy in fb_copies:
        copy.wait_recv()
    inv_loc.wait()
    wide = jnp.concatenate([fc[i] for i in range(16)], axis=1)
    piece = lax.dot_general(wide, invbuf[xlo], NT, preferred_element_type=f32).astype(bf16)
    my_rows = aligned(32 * r, 32)
    p0[s, z, my_rows, aligned(128 * xlo, 128)] = piece
    d1_copies = []
    for d in range(1, 16):
        slot = p0.at[s, z, my_rows, aligned(128 * xlo, 128)]
        d1_copies.append(rcopy(
            slot, slot, d1_send.at[d], d1_recv.at[d], (s, r, lax.rem(c + d, 16))
        ))
    for copy in d1_copies:
        copy.start()

    inv_rem.wait_recv()
    other_half = invbuf.at[1 - xlo, inv_half]
    inv_share = rcopy(other_half, other_half, x_send.at[2], x_recv.at[2], cpart)
    inv_share.start()
    ring_c.arrive(0)
    ring_c.start(1)

    rp_copies = [
        rcopy(fbuf.at[group, 0], fbuf.at[group, 0], rp_send.at[d], rp_recv.at[0], (s, r, d))
        for d in range(16)
    ]

    @pl.when(c == 0)
    def _():
        slot = fbuf.at[group, 0]
        rcopy(slot, slot, rs_send.at[0], rs_recv.at[0], xpart).wait_recv()
        for copy in rp_copies[1:]:
            copy.start()

    for copy in d1_copies:
        copy.wait_recv()
    spread_0 = Spread(
        lambda q: p0.at[s, :, aligned(32 * q, 32), :], d2_send, d2_recv, 4, y, core,
        lambda to: (s, 2 * to + core, c), cpart,
    )
    spread_0.start()
    ring_c.arrive(1)
    ring_c.start(2)
    for d in range(1, 4):
        spread_0.forward(d)
    ring_c.arrive(2)
    ring_c.start(3)

    slot = fbuf.at[group, 1]
    rcopy(slot, slot, cs_send.at[0], cs_recv.at[0], xpart).wait_recv()

    @pl.when(c != 0)
    def _():
        rp_copies[0].wait_recv()

    spread_f = Spread(
        lambda q: fbuf.at[q], kf_send, kf_recv, 8, chip, core,
        lambda to: at_group(2 * to + core), cpart,
    )
    spread_f.start()
    spread_0.finish()

    def product(left, right):
        total = jnp.zeros((256, 256), f32)
        for kz in range(8):
            total = total + lax.dot_general(
                left(kz), right(kz), NT, preferred_element_type=f32
            )
        return total

    tbuf[s] = product(lambda kz: p0[s, kz], lambda kz: p0[s, kz])
    t_parts = [tbuf.at[s, pl.ds(128, 128)], tbuf.at[s, pl.ds(0, 128), pl.ds(0, 128)]]
    t_copies = [rcopy(t_parts[i], t_parts[i], t_send.at[i], t_recv.at[i], hpart) for i in range(2)]
    for copy in t_copies:
        copy.start()

    inv_share.wait_recv()
    ring_c.arrive(3)
    for half in range(2):
        total = jnp.zeros((256, 128), f32)
        for kz in range(8):
            for kh in range(2):
                total = total + lax.dot_general(
                    cbuf[kz, kh],
                    invbuf[half, :, (kh * 8 + kz) * 128 : (kh * 8 + kz + 1) * 128],
                    NT,
                    preferred_element_type=f32,
                )
        ptile[:, 128 * half : 128 * half + 128] = total.astype(bf16)

    own_copies = []
    for xh in range(2):
        slot = prow.at[z, s]
        own_copies.append((
            same(pr_dest[xh]), rcopy(ptile, slot, pr_send.at[xh], pr_recv.at[s], pr_dest[xh]),
            slot, pr_recv.at[s],
        ))
    slot = pcol.at[2 * z + s]
    own_copies.append((
        same(pc_dest), rcopy(ptile, slot, pc_send.at[0], pc_recv.at[0], pc_dest),
        slot, pc_recv.at[0],
    ))
    for own, rem, slot, sem in own_copies:
        @pl.when(own)
        def _():
            pltpu.make_async_copy(ptile, slot, sem).start()

        @pl.when(jnp.logical_not(own))
        def _():
            rem.start()

    for d in range(1, 8):
        spread_f.forward(d)

    for child in range(2):
        slot = prow.at[z, child]
        rcopy(slot, slot, pr_send.at[0], pr_recv.at[child], xpart).wait_recv()
    ring_p = Ring(prow, p_send, p_recv, s, r, xlo, z)
    ring_p.start(0)
    rcopy(pcol.at[group], pcol.at[group], pc_send.at[0], pc_recv.at[0], xpart).wait_recv()
    spread_p = Spread(
        lambda q: pcol.at[q], k1_send, k1_recv, 8, chip, core,
        lambda to: at_group(2 * to + core), cpart,
    )
    spread_p.start()
    spread_f.finish()
    for copy in t_copies:
        copy.wait()

    @pl.when(r != 0)
    def _():
        u_start(u_copies[0])

    u_start(u_copies[1])
    p0_half = aligned(4 * core, 4)
    e_half = rcopy(p0.at[s, p0_half], p0.at[s, p0_half], e_send.at[0], e_recv.at[0], hpart)
    e_half.start()
    e_got = p0.at[1 - s, p0_half]
    e_share = rcopy(e_got, e_got, e_send.at[1], e_recv.at[1], cpart)
    ring_g = Ring(gbuf, g_send, g_recv, s, r, xlo, z)
    rcopy(gbuf.at[z], gbuf.at[z], gs_send.at[0], gs_recv.at[0], xpart).wait_recv()
    ring_g.start(0)

    @pl.when(root)
    def _():
        lead[...] = tile[...]

    @pl.when(jnp.logical_not(root))
    def _():
        for q in range(16):
            lead[32 * q : 32 * q + 32, :] = fbuf[q, 0].astype(f32)

    for child in range(2):
        for i in range(2):
            w = (map_ref[child, 0] == i).astype(f32)
            o = 256 * i
            at = (slice(o, o + 128), slice(o, o + 128))
            lead[at] = lead[at] - w * tbuf[child, 0:128, 0:128]
            at = (slice(o + 128, o + 256), slice(o, o + 256))
            lead[at] = lead[at] - w * tbuf[child, 128:256, :]

    @pl.loop(0, 4)
    def _(kb):
        at = aligned(kb * 128, 128)
        left, right = pivot_block(lead[at, at])
        for i in range(16):
            ut[8 * i : 8 * i + 8, :] = left[i]
            vt[kb, 8 * i : 8 * i + 8, :] = right[i]
        ring_p.arrive(kb)
        ring_g.arrive(kb)

        @pl.when(kb < 3)
        def _():
            ring_p.start(kb + 1)
            ring_g.start(kb + 1)
            spread_p.forward(2 * kb + 1)
            spread_p.forward(2 * kb + 2)

        @pl.when(kb == 3)
        def _():
            spread_p.forward(7)

        @pl.when(kb == 1)
        def _():
            e_half.wait_recv()
            e_share.start()

        row_id = lax.broadcasted_iota(jnp.int32, (512, 128), 0)
        panel = hdot(lead[:, at], vt[kb], NT)
        panel = jnp.where(row_id >= (kb + 1) * 128, panel, 0.0)
        lead[...] = lead[...] - hdot(panel, panel, NT)
        lead[:, at] = panel
        lead[at, at] = ut[...].T

    spread_p.finish()
    e_share.wait_recv()

    @pl.when(jnp.logical_not(leads))
    def _():
        own_entries()

    for h in range(8):
        both[64 * h : 64 * h + 64, 0:512] = gbuf[h].astype(f32)
        both[64 * h : 64 * h + 32, 512:1024] = fbuf[2 * h, 1].astype(f32)
        both[64 * h + 32 : 64 * h + 64, 512:1024] = fbuf[2 * h + 1, 1].astype(f32)
    for child in range(2):
        schur = product(lambda kz: prow[kz, child], lambda kz: pcol[2 * kz + child])
        row_part = product(lambda kz: p0[child, kz], lambda kz: prow[kz, child])
        col_part = product(lambda kz: p0[child, kz], lambda kz: pcol[2 * kz + child])
        lo = map_ref[child, 0]
        ro = map_ref[child, group] - 2 * group
        co = map_ref[child, c] - 2 * c
        for i in range(2):
            w = (lo == i).astype(f32)
            for k in range(2):
                tile[quarter(i, k)] = tile[quarter(i, k)] - weight(child, i, k) * schur
                at = quarter(i, k)
                both[at] = both[at] - w * (ro == k).astype(f32) * row_part
                at = quarter(i, k + 2)
                both[at] = both[at] - w * (co == k).astype(f32) * col_part

    @pl.when(c == 0)
    def _():
        both[:, 0:512] = tile[...].T

    for kb in range(4):
        at = slice(128 * kb, 128 * kb + 128)
        done = hdot(vt[kb], both[at, :], NN)
        both[at, :] = done
        if kb < 3:
            below = slice(128 * kb + 128, 512)
            both[below, :] = both[below, :] - hdot(lead[below, at], done, NN)

    @pl.when(leads)
    def _():
        row_id = lax.broadcasted_iota(jnp.int32, (512, 512), 0)
        col_id = lax.broadcasted_iota(jnp.int32, (512, 512), 1)
        keep = jnp.logical_and(c == 0, col_id <= row_id)
        o_ref[...] = jnp.where(keep, lead[...], 0.0)

    @pl.when(jnp.logical_and(jnp.logical_not(leads), c == 0))
    def _():
        o_ref[...] = both[:, 0:512].T

    @pl.when(jnp.logical_and(jnp.logical_not(leads), c != 0))
    def _():
        o_ref[...] = tile[...] - hdot(both[:, 0:512], both[:, 512:1024], TN)

    @pl.when(r == 0)
    def _():
        for copy in fa_copies:
            copy.wait_send()

    @pl.when(root)
    def _():
        for copy in rs_copies[1:]:
            copy.wait_send()

    @pl.when(leads)
    def _():
        for copy in cs_copies[1:] + gs_copies[1:]:
            copy.wait_send()

        @pl.when(c != 0)
        def _():
            gs_copies[0].wait_send()

    @pl.when(c == 0)
    def _():
        for copy in rp_copies[1:]:
            copy.wait_send()

    for entry in u_copies + own_copies:
        @pl.when(jnp.logical_not(entry[0]))
        def _():
            entry[1].wait_send()

    for copy in fb_copies + d1_copies + [cpl_rem, inv_rem, inv_share, e_half, e_share]:
        copy.wait_send()
    for gather in (ring_c, ring_p, ring_g, spread_0, spread_f, spread_p):
        gather.drain()


def local(child_update, child_coupling, pivot_inverse, child_map, parent_front, block_pattern):
    vmem = pl.BlockSpec(memory_space=pltpu.VMEM)
    smem = pl.BlockSpec(memory_space=pltpu.SMEM)
    hbm = pl.BlockSpec(memory_space=pl.ANY)
    dma = pltpu.SemaphoreType.DMA

    def pair(n, m):
        return [dma((n,)), dma((m,))]

    return pl.pallas_call(
        kernel,
        out_shape=jax.ShapeDtypeStruct((512, 512), f32),
        in_specs=[smem, smem, hbm, hbm, hbm, hbm],
        out_specs=vmem,
        scratch_shapes=[
            pltpu.VMEM((2, 128, 2048), bf16),
            pltpu.VMEM((8, 2, 256, 128), bf16),
            pltpu.VMEM((256, 256), bf16),
            pltpu.VMEM((8, 2, 256, 256), bf16),
            pltpu.VMEM((16, 256, 256), bf16),
            pltpu.VMEM((2, 256, 256), f32),
            pltpu.VMEM((512, 512), f32),
            pltpu.VMEM((512, 512), f32),
            pltpu.VMEM((512, 512), bf16),
            pltpu.VMEM((16, 2, 32, 512), bf16),
            pltpu.VMEM((8, 64, 512), bf16),
            pltpu.VMEM((16, 32, 128), bf16),
            pltpu.VMEM((2, 8, 256, 256), bf16),
            pltpu.VMEM((2, 256, 256), f32),
            pltpu.VMEM((512, 512), f32),
            pltpu.VMEM((512, 1024), f32),
            pltpu.VMEM((128, 128), f32),
            pltpu.VMEM((4, 128, 128), f32),
            dma((3,)), *pair(8, 1), *pair(16, 16), *pair(16, 16), *pair(8, 8),
            *pair(2, 2), *pair(3, 3), *pair(2, 2), *pair(7, 7), *pair(7, 7),
            *pair(7, 7), *pair(2, 2), *pair(1, 1), *pair(16, 16), *pair(16, 16),
            *pair(16, 1), *pair(16, 1), *pair(16, 1), *pair(16, 1), *pair(2, 2),
        ],
        compiler_params=pltpu.CompilerParams(
            has_side_effects=True, collective_id=0, vmem_limit_bytes=60 * 1024 * 1024
        ),
        cost_estimate=pl.CostEstimate(
            flops=8_000_000_000, bytes_accessed=4_000_000, transcendentals=512
        ),
    )(child_map, block_pattern, child_update, child_coupling, pivot_inverse, parent_front)


def solution(mesh):
    return jax.shard_map(
        local,
        mesh=mesh,
        in_specs=(
            P("sub", "row", "col"),
            P("sub", "row", "col"),
            P("sub", "col", None),
            P(),
            P(("sub", "row"), "col"),
            P(("sub", "row"), "col"),
        ),
        out_specs=P(("sub", "row"), "col"),
        check_vma=False,
    )
```

time: 1300 us -> 156 us (0.12)
  the two profiles are of different devices: /device:TPU:1 before, /device:TPU:10 now
where the time goes in v2:
time: 156 us
  Pallas kernels  154 us (99%)
  local copies, waits for them, and re-layouts  2.26 us (1%)
    pallas_call x1, Pallas kernels, local(): pl.pallas_call(kernel, out_shape=jax.ShapeDtypeStruct((512, 512), f32), i...  154 us

profile of v2, /device:TPU:10, one launch (start us, length us, event | category | flops | bytes accessed | tf_op | source)
XLA Modules:
  0.0 155.8 jit_solution(11547401291886237171)
XLA Ops:
  0.0 153.5 %shard_map.64 = f32[512,512]{1,0:T(8,128)} custom-call(s32[2,16]{1,0:T(2,128)} %map_ref.1, s32[2,2]{1,0:T(2,128)} %pat_ref.1, f32[1,512,256]{2,1,0:T(8,128)} %upd_ref.1, bf16[1,512,128]{2,1,0:T(8,128)(2,1)} %cpl_ref.1, bf16[1,128,2048]{2,1,0:T(8,128)(2,1)} %inv_ref.1, f32[512,512]{1,0:T(8,128)} %front_ref.1), custom_call_target="tpu_custom_call" | custom-call | flops 8000000000 | bytes 4000000 | tf_op jit(solution)/shard_map/pallas_call | solution.py:610
  153.5 2.3 %copy.8 = f32[512,512]{1,0:T(8,128)} copy(f32[512,512]{1,0:T(8,128)} %shard_map.64) | data formatting | bytes 2097152

commit v3 on v2

--- a/solution.py
+++ b/solution.py
@@ -24,35 +24,48 @@
 
 
 class Ring:
-    def __init__(self, buf, send, recv, s, r, xlo, z):
-        self.buf, self.send, self.recv, self.z = buf, send, recv, z
+    def __init__(self, slot, send, recv, right_last, s, r, xlo, z):
+        self.slot, self.send, self.recv, self.z = slot, send, recv, z
+        self.right_last = right_last
         self.to_right = (s, r, xlo * 8 + lax.rem(z + 1, 8))
         self.to_left = (s, r, xlo * 8 + lax.rem(z + 7, 8))
 
     def right(self, t):
-        slot = self.buf.at[lax.rem(self.z - t + 8, 8)]
+        slot = self.slot(lax.rem(self.z - t + 8, 8))
         return rcopy(slot, slot, self.send.at[t], self.recv.at[t], self.to_right)
 
     def left(self, t):
-        slot = self.buf.at[lax.rem(self.z + t, 8)]
+        slot = self.slot(lax.rem(self.z + t, 8))
         return rcopy(slot, slot, self.send.at[4 + t], self.recv.at[4 + t], self.to_left)
 
     def both(self, t, act):
-        act(self.right(t))
+        long, short = (self.right, self.left) if self.right_last else (self.left, self.right)
+        act(long(t))
         if isinstance(t, int):
             if t < 3:
-                act(self.left(t))
+                act(short(t))
         else:
 
             @pl.when(t < 3)
             def _():
-                act(self.left(t))
+                act(short(t))
 
     def start(self, t):
         self.both(t, lambda copy: copy.start())
 
     def arrive(self, t):
         self.both(t, lambda copy: copy.wait_recv())
+
+    def step(self, t):
+        self.arrive(t)
+        if isinstance(t, int):
+            if t < 3:
+                self.start(t + 1)
+        else:
+
+            @pl.when(t < 3)
+            def _():
+                self.start(t + 1)
 
     def drain(self):
         for t in range(4):
@@ -101,7 +114,7 @@
     return jnp.broadcast_to(x[k : k + 1, :], (8, 128))
 
 
-def pivot_block(d):
+def pivot_block(d, hook):
     left = [d[8 * i : 8 * i + 8, :] for i in range(16)]
     rid = lax.broadcasted_iota(jnp.int32, (8, 128), 0)
     cid = lax.broadcasted_iota(jnp.int32, (8, 128), 1)
@@ -135,11 +148,23 @@
                 lo = lo - f * row_l[k]
                 ro = ro - f * row_r[k]
             left[i], right[i] = lo, ro
+        if b == 5:
+            hook()
     return left, right
 
 
+def halves(x):
+    high = x.astype(bf16)
+    return high, (x - high.astype(f32)).astype(bf16)
+
+
 def hdot(a, b, dims):
-    return lax.dot_general(a, b, dims, precision=lax.Precision.HIGHEST, preferred_element_type=f32)
+    (ah, al), (bh, bl) = halves(a), halves(b)
+
+    def part(x, y):
+        return lax.dot_general(x, y, dims, preferred_element_type=f32)
+
+    return part(ah, bh) + (part(ah, bl) + part(al, bh))
 
 
 def kernel(
@@ -254,8 +279,20 @@
 
     cpl_loc.wait()
     cpl_rem.wait_recv()
-    ring_c = Ring(cbuf, c_send, c_recv, s, r, xlo, z)
-    ring_c.start(0)
+    ring_c = [
+        Ring(lambda q, kh=kh: cbuf.at[q, kh], c_send.at[kh], c_recv.at[kh], kh == 0, s, r, xlo, z)
+        for kh in range(2)
+    ]
+    for ring in ring_c:
+        ring.start(0)
+
+    @pl.when(r != 0)
+    def _():
+        u_start(u_copies[0])
+
+    u_start(u_copies[1])
+    for ring in ring_c:
+        ring.step(0)
 
     def weight(child, i, k):
         ro = map_ref[child, group] - 2 * group
@@ -290,29 +327,6 @@
         rs_copies.append(rcopy(
             piece, fbuf.at[cp, 0], rs_send.at[cp], rs_recv.at[0], (cp // 8, cp % 8, 0)
         ))
-
-    @pl.when(leads)
-    def _():
-        own_entries()
-        fsrc[...] = tile[...].astype(bf16)
-
-        @pl.when(c == 0)
-        def _():
-            for copy in rs_copies[1:]:
-                copy.start()
-            pltpu.make_async_copy(fsrc.at[pl.ds(0, 32)], fbuf.at[0, 0], rs_recv.at[0]).start()
-            pltpu.make_async_copy(fsrc.at[pl.ds(0, 64)], gbuf.at[0], gs_recv.at[0]).start()
-
-        pltpu.make_async_copy(fsrc.at[pl.ds(0, 32)], fbuf.at[0, 1], cs_recv.at[0]).start()
-        for copy in cs_copies[1:]:
-            copy.start()
-
-        @pl.when(c != 0)
-        def _():
-            gs_copies[0].start()
-
-        for copy in gs_copies[1:]:
-            copy.start()
 
     for copy in fb_copies:
         copy.wait_recv()
@@ -330,25 +344,38 @@
     for copy in d1_copies:
         copy.start()
 
+    for ring in ring_c:
+        ring.step(1)
     inv_rem.wait_recv()
     other_half = invbuf.at[1 - xlo, inv_half]
     inv_share = rcopy(other_half, other_half, x_send.at[2], x_recv.at[2], cpart)
     inv_share.start()
-    ring_c.arrive(0)
-    ring_c.start(1)
-
-    rp_copies = [
-        rcopy(fbuf.at[group, 0], fbuf.at[group, 0], rp_send.at[d], rp_recv.at[0], (s, r, d))
-        for d in range(16)
-    ]
-
-    @pl.when(c == 0)
-    def _():
-        slot = fbuf.at[group, 0]
-        rcopy(slot, slot, rs_send.at[0], rs_recv.at[0], xpart).wait_recv()
-        for copy in rp_copies[1:]:
+
+    @pl.when(leads)
+    def _():
+        own_entries()
+        fsrc[...] = tile[...].astype(bf16)
+
+        @pl.when(c == 0)
+        def _():
+            for copy in rs_copies[1:]:
+                copy.start()
+            pltpu.make_async_copy(fsrc.at[pl.ds(0, 32)], fbuf.at[0, 0], rs_recv.at[0]).start()
+            pltpu.make_async_copy(fsrc.at[pl.ds(0, 64)], gbuf.at[0], gs_recv.at[0]).start()
+
+        pltpu.make_async_copy(fsrc.at[pl.ds(0, 32)], fbuf.at[0, 1], cs_recv.at[0]).start()
+        for copy in cs_copies[1:]:
             copy.start()
 
+        @pl.when(c != 0)
+        def _():
+            gs_copies[0].start()
+
+        for copy in gs_copies[1:]:
+            copy.start()
+
+    for ring in ring_c:
+        ring.step(2)
     for copy in d1_copies:
         copy.wait_recv()
     spread_0 = Spread(
@@ -356,53 +383,25 @@
         lambda to: (s, 2 * to + core, c), cpart,
     )
     spread_0.start()
-    ring_c.arrive(1)
-    ring_c.start(2)
-    for d in range(1, 4):
-        spread_0.forward(d)
-    ring_c.arrive(2)
-    ring_c.start(3)
-
-    slot = fbuf.at[group, 1]
-    rcopy(slot, slot, cs_send.at[0], cs_recv.at[0], xpart).wait_recv()
-
-    @pl.when(c != 0)
-    def _():
-        rp_copies[0].wait_recv()
-
-    spread_f = Spread(
-        lambda q: fbuf.at[q], kf_send, kf_recv, 8, chip, core,
-        lambda to: at_group(2 * to + core), cpart,
-    )
-    spread_f.start()
-    spread_0.finish()
-
-    def product(left, right):
-        total = jnp.zeros((256, 256), f32)
-        for kz in range(8):
-            total = total + lax.dot_general(
-                left(kz), right(kz), NT, preferred_element_type=f32
-            )
-        return total
-
-    tbuf[s] = product(lambda kz: p0[s, kz], lambda kz: p0[s, kz])
-    t_parts = [tbuf.at[s, pl.ds(128, 128)], tbuf.at[s, pl.ds(0, 128), pl.ds(0, 128)]]
-    t_copies = [rcopy(t_parts[i], t_parts[i], t_send.at[i], t_recv.at[i], hpart) for i in range(2)]
-    for copy in t_copies:
-        copy.start()
+
+    rp_copies = [
+        rcopy(fbuf.at[group, 0], fbuf.at[group, 0], rp_send.at[d], rp_recv.at[0], (s, r, d))
+        for d in range(16)
+    ]
+
+    @pl.when(c == 0)
+    def _():
+        slot = fbuf.at[group, 0]
+        rcopy(slot, slot, rs_send.at[0], rs_recv.at[0], xpart).wait_recv()
+        for copy in rp_copies[1:]:
+            copy.start()
 
     inv_share.wait_recv()
-    ring_c.arrive(3)
+    for ring in ring_c:
+        ring.step(3)
+    wide = jnp.concatenate([cbuf[q % 8, q // 8] for q in range(16)], axis=1)
     for half in range(2):
-        total = jnp.zeros((256, 128), f32)
-        for kz in range(8):
-            for kh in range(2):
-                total = total + lax.dot_general(
-                    cbuf[kz, kh],
-                    invbuf[half, :, (kh * 8 + kz) * 128 : (kh * 8 + kz + 1) * 128],
-                    NT,
-                    preferred_element_type=f32,
-                )
+        total = lax.dot_general(wide, invbuf[half], NT, preferred_element_type=f32)
         ptile[:, 128 * half : 128 * half + 128] = total.astype(bf16)
 
     own_copies = []
@@ -426,37 +425,67 @@
         def _():
             rem.start()
 
-    for d in range(1, 8):
-        spread_f.forward(d)
+    for d in range(1, 4):
+        spread_0.forward(d)
 
     for child in range(2):
         slot = prow.at[z, child]
         rcopy(slot, slot, pr_send.at[0], pr_recv.at[child], xpart).wait_recv()
-    ring_p = Ring(prow, p_send, p_recv, s, r, xlo, z)
-    ring_p.start(0)
+    ring_p = [
+        Ring(
+            lambda q, child=child: prow.at[q, child],
+            p_send.at[child], p_recv.at[child], child == 0, s, r, xlo, z,
+        )
+        for child in range(2)
+    ]
+    for ring in ring_p:
+        ring.start(0)
+    spread_0.finish()
+
+    def across(left, right):
+        return lax.dot_general(left, right, NT, preferred_element_type=f32)
+
+    def panel_0(child):
+        return jnp.concatenate([p0[child, kz] for kz in range(8)], axis=1)
+
+    wide = panel_0(s)
+    tbuf[s] = across(wide, wide)
+    t_parts = [tbuf.at[s, pl.ds(128, 128)], tbuf.at[s, pl.ds(0, 128), pl.ds(0, 128)]]
+    t_copies = [rcopy(t_parts[i], t_parts[i], t_send.at[i], t_recv.at[i], hpart) for i in range(2)]
+    for copy in t_copies:
+        copy.start()
+
+    slot = fbuf.at[group, 1]
+    rcopy(slot, slot, cs_send.at[0], cs_recv.at[0], xpart).wait_recv()
+
+    @pl.when(c != 0)
+    def _():
+        rp_copies[0].wait_recv()
+
+    spread_f = Spread(
+        lambda q: fbuf.at[q], kf_send, kf_recv, 8, chip, core,
+        lambda to: at_group(2 * to + core), cpart,
+    )
+    spread_f.start()
     rcopy(pcol.at[group], pcol.at[group], pc_send.at[0], pc_recv.at[0], xpart).wait_recv()
     spread_p = Spread(
         lambda q: pcol.at[q], k1_send, k1_recv, 8, chip, core,
         lambda to: at_group(2 * to + core), cpart,
     )
     spread_p.start()
-    spread_f.finish()
-    for copy in t_copies:
-        copy.wait()
-
-    @pl.when(r != 0)
-    def _():
-        u_start(u_copies[0])
-
-    u_start(u_copies[1])
     p0_half = aligned(4 * core, 4)
     e_half = rcopy(p0.at[s, p0_half], p0.at[s, p0_half], e_send.at[0], e_recv.at[0], hpart)
     e_half.start()
     e_got = p0.at[1 - s, p0_half]
     e_share = rcopy(e_got, e_got, e_send.at[1], e_recv.at[1], cpart)
-    ring_g = Ring(gbuf, g_send, g_recv, s, r, xlo, z)
+    ring_g = Ring(lambda q: gbuf.at[q], g_send, g_recv, True, s, r, xlo, z)
     rcopy(gbuf.at[z], gbuf.at[z], gs_send.at[0], gs_recv.at[0], xpart).wait_recv()
     ring_g.start(0)
+    for d in range(1, 8):
+        spread_f.forward(d)
+    spread_f.finish()
+    for copy in t_copies:
+        copy.wait()
 
     @pl.when(root)
     def _():
@@ -479,17 +508,15 @@
     @pl.loop(0, 4)
     def _(kb):
         at = aligned(kb * 128, 128)
-        left, right = pivot_block(lead[at, at])
+        left, right = pivot_block(lead[at, at], lambda: ring_p[0].step(kb))
         for i in range(16):
             ut[8 * i : 8 * i + 8, :] = left[i]
             vt[kb, 8 * i : 8 * i + 8, :] = right[i]
-        ring_p.arrive(kb)
-        ring_g.arrive(kb)
+        ring_p[1].step(kb)
+        ring_g.step(kb)
 
         @pl.when(kb < 3)
         def _():
-            ring_p.start(kb + 1)
-            ring_g.start(kb + 1)
             spread_p.forward(2 * kb + 1)
             spread_p.forward(2 * kb + 2)
 
@@ -501,6 +528,13 @@
         def _():
             e_half.wait_recv()
             e_share.start()
+
+            @pl.when(jnp.logical_not(leads))
+            def _():
+                own_entries()
+
+            for q in range(16):
+                both[32 * q : 32 * q + 32, 512:1024] = fbuf[q, 1].astype(f32)
 
         row_id = lax.broadcasted_iota(jnp.int32, (512, 128), 0)
         panel = hdot(lead[:, at], vt[kb], NT)
@@ -511,19 +545,15 @@
 
     spread_p.finish()
     e_share.wait_recv()
-
-    @pl.when(jnp.logical_not(leads))
-    def _():
-        own_entries()
-
     for h in range(8):
         both[64 * h : 64 * h + 64, 0:512] = gbuf[h].astype(f32)
-        both[64 * h : 64 * h + 32, 512:1024] = fbuf[2 * h, 1].astype(f32)
-        both[64 * h + 32 : 64 * h + 64, 512:1024] = fbuf[2 * h + 1, 1].astype(f32)
     for child in range(2):
-        schur = product(lambda kz: prow[kz, child], lambda kz: pcol[2 * kz + child])
-        row_part = product(lambda kz: p0[child, kz], lambda kz: prow[kz, child])
-        col_part = product(lambda kz: p0[child, kz], lambda kz: pcol[2 * kz + child])
+        here = jnp.concatenate([prow[kz, child] for kz in range(8)], axis=1)
+        there = jnp.concatenate([pcol[2 * kz + child] for kz in range(8)], axis=1)
+        first = panel_0(child)
+        schur = across(here, there)
+        row_part = across(first, here)
+        col_part = across(first, there)
         lo = map_ref[child, 0]
         ro = map_ref[child, group] - 2 * group
         co = map_ref[child, c] - 2 * c
@@ -594,7 +624,7 @@
 
     for copy in fb_copies + d1_copies + [cpl_rem, inv_rem, inv_share, e_half, e_share]:
         copy.wait_send()
-    for gather in (ring_c, ring_p, ring_g, spread_0, spread_f, spread_p):
+    for gather in (*ring_c, *ring_p, ring_g, spread_0, spread_f, spread_p):
         gather.drain()
 
 
@@ -632,8 +662,8 @@
             pltpu.VMEM((128, 128), f32),
             pltpu.VMEM((4, 128, 128), f32),
             dma((3,)), *pair(8, 1), *pair(16, 16), *pair(16, 16), *pair(8, 8),
-            *pair(2, 2), *pair(3, 3), *pair(2, 2), *pair(7, 7), *pair(7, 7),
-            *pair(7, 7), *pair(2, 2), *pair(1, 1), *pair(16, 16), *pair(16, 16),
+            *pair(2, 2), *pair(3, 3), *pair(2, 2), dma((2, 8)), dma((2, 8)), dma((2, 8)), dma((2, 8)),
+            *pair(8, 8), *pair(2, 2), *pair(1, 1), *pair(16, 16), *pair(16, 16),
             *pair(16, 1), *pair(16, 1), *pair(16, 1), *pair(16, 1), *pair(2, 2),
         ],
         compiler_params=pltpu.CompilerParams(

time: 156 us -> 120 us (0.77)
  the two profiles are of different devices: /device:TPU:10 before, /device:TPU:9 now
where the time goes in v3:
time: 120 us
  Pallas kernels  117 us (98%)
  local copies, waits for them, and re-layouts  2.26 us (2%)
    pallas_call x1, Pallas kernels, local(): pl.pallas_call(kernel, out_shape=jax.ShapeDtypeStruct((512, 512), f32), i...  117 us

profile of v3, /device:TPU:9, one launch (start us, length us, event | category | flops | bytes accessed | tf_op | source)
XLA Modules:
  0.0 119.7 jit_solution(2016393759930319146)
XLA Ops:
  0.0 117.5 %shard_map.64 = f32[512,512]{1,0:T(8,128)} custom-call(s32[2,16]{1,0:T(2,128)} %map_ref.1, s32[2,2]{1,0:T(2,128)} %pat_ref.1, f32[1,512,256]{2,1,0:T(8,128)} %upd_ref.1, bf16[1,512,128]{2,1,0:T(8,128)(2,1)} %cpl_ref.1, bf16[1,128,2048]{2,1,0:T(8,128)(2,1)} %inv_ref.1, f32[512,512]{1,0:T(8,128)} %front_ref.1), custom_call_target="tpu_custom_call" | custom-call | flops 8000000000 | bytes 4000000 | tf_op jit(solution)/shard_map/pallas_call | solution.py:640
  117.5 2.3 %copy.8 = f32[512,512]{1,0:T(8,128)} copy(f32[512,512]{1,0:T(8,128)} %shard_map.64) | data formatting | bytes 2097152

commit v4 on v3

--- a/solution.py
+++ b/solution.py
@@ -73,6 +73,59 @@
 
 
 class Spread:
+    def __init__(self, slot, send, recv, s, r, c):
+        self.slot, self.send, self.recv = slot, send, recv
+        self.s, self.r, self.c = s, r, c
+        self.y, self.core = r // 2, lax.rem(r, 2)
+
+    def piece(self, side, back):
+        side = self.s if side == 0 else 1 - self.s
+        return self.slot(side, 2 * lax.rem(self.y - back + 4, 4) + self.core)
+
+    def copy(self, ref, sem, dev):
+        return rcopy(ref, ref, self.send.at[sem], self.recv.at[sem], dev)
+
+    def hop(self):
+        return self.copy(self.piece(0, 0), 0, (1 - self.s, self.r, self.c))
+
+    def along(self, side, d):
+        to = (self.s, 2 * lax.rem(self.y + d, 4) + self.core, self.c)
+        return self.copy(self.piece(side, 0), 3 * side + d, to)
+
+    def share(self, side, d):
+        to = (self.s, self.r + 1 - 2 * self.core, self.c)
+        return self.copy(self.piece(side, d), 7 + 4 * side + d, to)
+
+    def start(self):
+        for d in range(1, 4):
+            self.along(0, d).start()
+        self.share(0, 0).start()
+
+    def relay(self):
+        self.hop().wait_recv()
+        for d in range(1, 4):
+            self.along(1, d).start()
+        self.share(1, 0).start()
+
+    def forward(self, side):
+        for d in range(1, 4):
+            self.along(side, d).wait_recv()
+            self.share(side, d).start()
+
+    def finish(self, side):
+        for d in range(4):
+            self.share(side, d).wait_recv()
+
+    def drain(self):
+        self.hop().wait_send()
+        for side in range(2):
+            for d in range(4):
+                if d:
+                    self.along(side, d).wait_send()
+                self.share(side, d).wait_send()
+
+
+class Direct:
     def __init__(self, slot, send, recv, n, chip, core, device, partner):
         self.slot, self.send, self.recv, self.n = slot, send, recv, n
         self.chip, self.core, self.device, self.partner = chip, core, device, partner
@@ -174,7 +227,7 @@
     loc_sem, fa_send, fa_recv, fb_send, fb_recv, d1_send, d1_recv, d2_send, d2_recv,
     t_send, t_recv, x_send, x_recv, u_send, u_recv, c_send, c_recv, p_send, p_recv,
     g_send, g_recv, pr_send, pr_recv, pc_send, pc_recv, k1_send, k1_recv, kf_send, kf_recv,
-    rs_send, rs_recv, rp_send, rp_recv, gs_send, gs_recv, cs_send, cs_recv, e_send, e_recv,
+    rs_send, rs_recv, rp_send, rp_recv, gs_send, gs_recv, cs_send, cs_recv,
 ):
     s, r, c = lax.axis_index("sub"), lax.axis_index("row"), lax.axis_index("col")
     xlo, z = c // 8, lax.rem(c, 8)
@@ -379,8 +432,7 @@
     for copy in d1_copies:
         copy.wait_recv()
     spread_0 = Spread(
-        lambda q: p0.at[s, :, aligned(32 * q, 32), :], d2_send, d2_recv, 4, y, core,
-        lambda to: (s, 2 * to + core, c), cpart,
+        lambda side, q: p0.at[side, :, aligned(32 * q, 32), :], d2_send, d2_recv, s, r, c
     )
     spread_0.start()
 
@@ -425,8 +477,34 @@
         def _():
             rem.start()
 
-    for d in range(1, 4):
-        spread_0.forward(d)
+    spread_0.forward(0)
+    spread_0.finish(0)
+
+    def across(left, right):
+        return lax.dot_general(left, right, NT, preferred_element_type=f32)
+
+    def panel_0(child):
+        return jnp.concatenate([p0[child, kz] for kz in range(8)], axis=1)
+
+    wide = panel_0(s)
+    tbuf[s] = across(wide, wide)
+    t_parts = [tbuf.at[s, pl.ds(128, 128)], tbuf.at[s, pl.ds(0, 128), pl.ds(0, 128)]]
+    t_copies = [rcopy(t_parts[i], t_parts[i], t_send.at[i], t_recv.at[i], hpart) for i in range(2)]
+    for copy in t_copies:
+        copy.start()
+
+    slot = fbuf.at[group, 1]
+    rcopy(slot, slot, cs_send.at[0], cs_recv.at[0], xpart).wait_recv()
+
+    @pl.when(c != 0)
+    def _():
+        rp_copies[0].wait_recv()
+
+    spread_f = Direct(
+        lambda q: fbuf.at[q], kf_send, kf_recv, 8, chip, core,
+        lambda to: at_group(2 * to + core), cpart,
+    )
+    spread_f.start()
 
     for child in range(2):
         slot = prow.at[z, child]
@@ -440,44 +518,11 @@
     ]
     for ring in ring_p:
         ring.start(0)
-    spread_0.finish()
-
-    def across(left, right):
-        return lax.dot_general(left, right, NT, preferred_element_type=f32)
-
-    def panel_0(child):
-        return jnp.concatenate([p0[child, kz] for kz in range(8)], axis=1)
-
-    wide = panel_0(s)
-    tbuf[s] = across(wide, wide)
-    t_parts = [tbuf.at[s, pl.ds(128, 128)], tbuf.at[s, pl.ds(0, 128), pl.ds(0, 128)]]
-    t_copies = [rcopy(t_parts[i], t_parts[i], t_send.at[i], t_recv.at[i], hpart) for i in range(2)]
-    for copy in t_copies:
-        copy.start()
-
-    slot = fbuf.at[group, 1]
-    rcopy(slot, slot, cs_send.at[0], cs_recv.at[0], xpart).wait_recv()
-
-    @pl.when(c != 0)
-    def _():
-        rp_copies[0].wait_recv()
-
-    spread_f = Spread(
-        lambda q: fbuf.at[q], kf_send, kf_recv, 8, chip, core,
-        lambda to: at_group(2 * to + core), cpart,
-    )
-    spread_f.start()
     rcopy(pcol.at[group], pcol.at[group], pc_send.at[0], pc_recv.at[0], xpart).wait_recv()
-    spread_p = Spread(
-        lambda q: pcol.at[q], k1_send, k1_recv, 8, chip, core,
-        lambda to: at_group(2 * to + core), cpart,
-    )
+    spread_p = Spread(lambda side, q: pcol.at[8 * side + q], k1_send, k1_recv, s, r, c)
+    spread_p.hop().start()
     spread_p.start()
-    p0_half = aligned(4 * core, 4)
-    e_half = rcopy(p0.at[s, p0_half], p0.at[s, p0_half], e_send.at[0], e_recv.at[0], hpart)
-    e_half.start()
-    e_got = p0.at[1 - s, p0_half]
-    e_share = rcopy(e_got, e_got, e_send.at[1], e_recv.at[1], cpart)
+    spread_0.hop().start()
     ring_g = Ring(lambda q: gbuf.at[q], g_send, g_recv, True, s, r, xlo, z)
     rcopy(gbuf.at[z], gbuf.at[z], gs_send.at[0], gs_recv.at[0], xpart).wait_recv()
     ring_g.start(0)
@@ -486,6 +531,7 @@
     spread_f.finish()
     for copy in t_copies:
         copy.wait()
+    spread_p.relay()
 
     @pl.when(root)
     def _():
@@ -515,19 +561,15 @@
         ring_p[1].step(kb)
         ring_g.step(kb)
 
-        @pl.when(kb < 3)
-        def _():
-            spread_p.forward(2 * kb + 1)
-            spread_p.forward(2 * kb + 2)
-
-        @pl.when(kb == 3)
-        def _():
-            spread_p.forward(7)
+        @pl.when(kb == 0)
+        def _():
+            spread_p.forward(0)
+            spread_0.relay()
 
         @pl.when(kb == 1)
         def _():
-            e_half.wait_recv()
-            e_share.start()
+            spread_p.forward(1)
+            spread_0.forward(1)
 
             @pl.when(jnp.logical_not(leads))
             def _():
@@ -543,8 +585,9 @@
         lead[:, at] = panel
         lead[at, at] = ut[...].T
 
-    spread_p.finish()
-    e_share.wait_recv()
+    for side in range(2):
+        spread_p.finish(side)
+    spread_0.finish(1)
     for h in range(8):
         both[64 * h : 64 * h + 64, 0:512] = gbuf[h].astype(f32)
     for child in range(2):
@@ -622,7 +665,7 @@
         def _():
             entry[1].wait_send()
 
-    for copy in fb_copies + d1_copies + [cpl_rem, inv_rem, inv_share, e_half, e_share]:
+    for copy in fb_copies + d1_copies + [cpl_rem, inv_rem, inv_share]:
         copy.wait_send()
     for gather in (*ring_c, *ring_p, ring_g, spread_0, spread_f, spread_p):
         gather.drain()
@@ -661,10 +704,10 @@
             pltpu.VMEM((512, 1024), f32),
             pltpu.VMEM((128, 128), f32),
             pltpu.VMEM((4, 128, 128), f32),
-            dma((3,)), *pair(8, 1), *pair(16, 16), *pair(16, 16), *pair(8, 8),
+            dma((3,)), *pair(8, 1), *pair(16, 16), *pair(16, 16), *pair(15, 15),
             *pair(2, 2), *pair(3, 3), *pair(2, 2), dma((2, 8)), dma((2, 8)), dma((2, 8)), dma((2, 8)),
             *pair(8, 8), *pair(2, 2), *pair(1, 1), *pair(16, 16), *pair(16, 16),
-            *pair(16, 1), *pair(16, 1), *pair(16, 1), *pair(16, 1), *pair(2, 2),
+            *pair(16, 1), *pair(16, 1), *pair(16, 1), *pair(16, 1),
         ],
         compiler_params=pltpu.CompilerParams(
             has_side_effects=True, collective_id=0, vmem_limit_bytes=60 * 1024 * 1024

time: 120 us -> 105 us (0.88)
  the two profiles are of different devices: /device:TPU:9 before, /device:TPU:1 now
where the time goes in v4:
time: 105 us
  Pallas kernels  103 us (98%)
  local copies, waits for them, and re-layouts  2.26 us (2%)
    pallas_call x1, Pallas kernels, local(): pl.pallas_call(kernel, out_shape=jax.ShapeDtypeStruct((512, 512), f32), i...  103 us
    unnamed x1, local copies, waits for them, and re-layouts  2.26 us

profile of v4, /device:TPU:1, one launch (start us, length us, event | category | flops | bytes accessed | tf_op | source)
XLA Modules:
  0.0 104.9 jit_solution(2796796682344649615)
XLA Ops:
  0.0 102.6 %shard_map.64 = f32[512,512]{1,0:T(8,128)} custom-call(s32[2,16]{1,0:T(2,128)} %map_ref.1, s32[2,2]{1,0:T(2,128)} %pat_ref.1, f32[1,512,256]{2,1,0:T(8,128)} %upd_ref.1, bf16[1,512,128]{2,1,0:T(8,128)(2,1)} %cpl_ref.1, bf16[1,128,2048]{2,1,0:T(8,128)(2,1)} %inv_ref.1, f32[512,512]{1,0:T(8,128)} %front_ref.1), custom_call_target="tpu_custom_call" | custom-call | flops 8000000000 | bytes 4000000 | tf_op jit(solution)/shard_map/pallas_call | solution.py:683
  102.6 2.3 %copy.8 = f32[512,512]{1,0:T(8,128)} copy(f32[512,512]{1,0:T(8,128)} %shard_map.64) | data formatting | bytes 2097152

commit v5 on v4

--- a/solution.py
+++ b/solution.py
@@ -478,6 +478,9 @@
             rem.start()
 
     spread_0.forward(0)
+    ring_g = Ring(lambda q: gbuf.at[q], g_send, g_recv, True, s, r, xlo, z)
+    rcopy(gbuf.at[z], gbuf.at[z], gs_send.at[0], gs_recv.at[0], xpart).wait_recv()
+    ring_g.start(0)
     spread_0.finish(0)
 
     def across(left, right):
@@ -523,15 +526,14 @@
     spread_p.hop().start()
     spread_p.start()
     spread_0.hop().start()
-    ring_g = Ring(lambda q: gbuf.at[q], g_send, g_recv, True, s, r, xlo, z)
-    rcopy(gbuf.at[z], gbuf.at[z], gs_send.at[0], gs_recv.at[0], xpart).wait_recv()
-    ring_g.start(0)
+    ring_g.step(0)
     for d in range(1, 8):
         spread_f.forward(d)
     spread_f.finish()
     for copy in t_copies:
         copy.wait()
     spread_p.relay()
+    ring_g.step(1)
 
     @pl.when(root)
     def _():
@@ -559,16 +561,23 @@
             ut[8 * i : 8 * i + 8, :] = left[i]
             vt[kb, 8 * i : 8 * i + 8, :] = right[i]
         ring_p[1].step(kb)
-        ring_g.step(kb)
-
-        @pl.when(kb == 0)
+
+        @pl.when(kb < 2)
+        def _():
+            ring_g.step(kb + 2)
+
+
+        @pl.when(kb == 1)
         def _():
             spread_p.forward(0)
             spread_0.relay()
 
-        @pl.when(kb == 1)
+        @pl.when(kb == 2)
         def _():
             spread_p.forward(1)
+
+        @pl.when(kb == 3)
+        def _():
             spread_0.forward(1)
 
             @pl.when(jnp.logical_not(leads))

time: 105 us -> 104 us (level)
  the two profiles are of different devices: /device:TPU:1 before, /device:TPU:37 now
where the time goes in v5:
time: 104 us
  Pallas kernels  101 us (97%)
  local copies, waits for them, and re-layouts  2.26 us (2%)
    pallas_call x1, Pallas kernels, local(): pl.pallas_call(kernel, out_shape=jax.ShapeDtypeStruct((512, 512), f32), i...  101 us
    unnamed x1, local copies, waits for them, and re-layouts  2.26 us

profile of v5, /device:TPU:37, one launch (start us, length us, event | category | flops | bytes accessed | tf_op | source)
XLA Modules:
  0.0 103.6 jit_solution(3117109823096924255)
XLA Ops:
  0.0 101.4 %shard_map.64 = f32[512,512]{1,0:T(8,128)} custom-call(s32[2,16]{1,0:T(2,128)} %map_ref.1, s32[2,2]{1,0:T(2,128)} %pat_ref.1, f32[1,512,256]{2,1,0:T(8,128)} %upd_ref.1, bf16[1,512,128]{2,1,0:T(8,128)(2,1)} %cpl_ref.1, bf16[1,128,2048]{2,1,0:T(8,128)(2,1)} %inv_ref.1, f32[512,512]{1,0:T(8,128)} %front_ref.1), custom_call_target="tpu_custom_call" | custom-call | flops 8000000000 | bytes 4000000 | tf_op jit(solution)/shard_map/pallas_call | solution.py:692
  101.4 2.3 %copy.8 = f32[512,512]{1,0:T(8,128)} copy(f32[512,512]{1,0:T(8,128)} %shard_map.64) | data formatting | bytes 2097152
